TPU v7x, 512 devices: a whole 4x8x8 slice. The times are simulated.
512 devices in a mesh: raster: 32 (over x, y), slit: 16 (over z, core).
Axes of the slice: x: 4, y: 8, z: 8, core: 2. Of those that a mesh axis runs over, the one named last changes fastest.
Arguments:
- spectra: float32 [1048576, 512], P(('raster', 'slit')), as said below
- start: float32 [512, 64], replicated, may hold values from -0.25 to 0.25
Outputs:
- coefficients: float32 [1048576, 64], P(('raster', 'slit'))
Inputs may be any that keep to these rules, and one draw needn't show every extreme that they name: `spectra`: every spectrum is a real-valued row of order one; the columns of every device's block are linearly independent.
All inputs are finite; a program needn't handle non-finite values.
Results may differ from a plain program's by a relative error of at most 0.0003.
Values sent between devices are 32-bit elements; how exact they have to be, the bound alone decides.
No kernel may reach another device: no remote copies, remote signals or barrier semaphores. Data moves between devices by JAX's collectives and lax.ppermute only.
A program may use at most 128 MiB of HBM per device.

v0:
```python
import jax
import jax.numpy as jnp
from jax import lax
from jax.sharding import PartitionSpec as P

ITERS = 6


def cross_of(matrix):
    return jnp.dot(
        matrix.T, matrix, precision=lax.Precision.HIGHEST, preferred_element_type=jnp.float32
    )


def orthonormal(image):
    lower = jnp.linalg.cholesky(cross_of(image))
    return lax.linalg.triangular_solve(lower, image, left_side=False, lower=True, transpose_a=True)


def body(spectra, start):
    local_gram = cross_of(spectra)
    gram = lax.psum(local_gram, ("raster", "slit"))
    upper = jnp.linalg.cholesky(gram).T
    basis = start
    for step in range(ITERS):
        inner = jnp.dot(
            upper, basis, precision=lax.Precision.HIGHEST, preferred_element_type=jnp.float32
        )
        image = jnp.dot(
            upper.T, inner, precision=lax.Precision.HIGHEST, preferred_element_type=jnp.float32
        )
        basis = orthonormal(image)
    return jnp.dot(
        spectra, basis, precision=lax.Precision.HIGHEST, preferred_element_type=jnp.float32
    )


def solution(mesh):
    placed = (P(("raster", "slit"), None), P())
    return jax.shard_map(
        body, mesh=mesh, in_specs=placed, out_specs=P(("raster", "slit"), None), check_vma=False
    )
```

profile of v0, /device:TPU:1, one launch (start us, length us, event | category | flops | bytes accessed | tf_op | source)
XLA Modules:
  0.0 487.0 jit_solution(5884154429861132300)
XLA Ops:
  6.5 11.5 %fusion.52 = f32[512,512]{0,1:T(8,128)} fusion(f32[2048,512]{1,0:T(8,128)} %param.5), kind=kOutput, calls=%fused_computation.105 | convolution fusion | flops 6442450944 | bytes 5242880 | tf_op jit(solution)/shard_map/dot_general | solution.py:10
  18.1 278.2 %all-reduce.3.cloned.1.call-done = f32[512,512]{0,1:T(8,128)} async-done(((f32[512,512]{0,1:T(8,128)}), f32[512,512]{0,1:T(8,128)}) %all-reduce.3.cloned.1.call-update) | async-done | bytes 1048592 | tf_op jit(solution)/shard_map/psum | solution.py:22
  296.3 1.6 copy.4
  297.8 1.4 fusion
  299.3 11.7 %cholesky.120 = f32[128,128]{1,0:T(8,128)S(1)} custom-call(f32[128,128]{1,0:T(8,128)S(1)} %cholesky.434), custom_call_target="Cholesky" | custom-call | tf_op jit(solution)/shard_map/jit(cholesky)/cholesky | solution.py:23
  311.1 9.8 %custom-call.32 = f32[1,128,128]{1,2,0:T(8,128)S(1)} custom-call(f32[1,128,128]{2,1,0:T(8,128)S(1)} %get-tuple-element.16), custom_call_target="InvertDiagBlocksLowerTriangular" | custom-call | tf_op jit(solution)/shard_map/jit(cholesky)/cholesky | solution.py:23
  321.0 0.3 constant_dynamic-update-slice_fusion.2
  321.3 0.3 convolution_subtract_fusion
  321.7 11.7 %cholesky.244 = f32[128,128]{1,0:T(8,128)S(1)} custom-call(f32[128,128]{1,0:T(8,128)S(1)} %cholesky.438), custom_call_target="Cholesky" | custom-call | tf_op jit(solution)/shard_map/jit(cholesky)/cholesky | solution.py:23
  333.4 10.0 %custom-call.33 = f32[1,128,128]{1,2,0:T(8,128)S(1)} custom-call(f32[1,128,128]{2,1,0:T(8,128)S(1)} %get-tuple-element.13), custom_call_target="InvertDiagBlocksLowerTriangular" | custom-call | tf_op jit(solution)/shard_map/jit(cholesky)/cholesky | solution.py:23
  343.7 0.4 convolution_subtract_fusion.1
  344.1 11.7 %cholesky.265 = f32[128,128]{1,0:T(8,128)S(1)} custom-call(f32[128,128]{1,0:T(8,128)S(1)} %cholesky.443), custom_call_target="Cholesky" | custom-call | tf_op jit(solution)/shard_map/jit(cholesky)/cholesky | solution.py:23
  355.8 0.7 compare_reduce_fusion.7
  356.6 9.8 %custom-call.34 = f32[1,128,128]{1,2,0:T(8,128)S(1)} custom-call(f32[1,128,128]{2,1,0:T(8,128)S(1)} %get-tuple-element.10), custom_call_target="InvertDiagBlocksLowerTriangular" | custom-call | tf_op jit(solution)/shard_map/jit(cholesky)/cholesky | solution.py:23
  366.6 0.4 convolution_subtract_fusion.2
  367.0 11.7 %cholesky.282 = f32[128,128]{1,0:T(8,128)S(1)} custom-call(f32[128,128]{1,0:T(8,128)S(1)} %convolution_subtract_fusion.2), custom_call_target="Cholesky" | custom-call | tf_op jit(solution)/shard_map/jit(cholesky)/cholesky | solution.py:23
  378.7 0.6 compare_reduce_fusion.6
  379.4 0.7 compare_reduce_fusion.8
  382.6 1.6 fusion.51
  384.2 0.9 fusion.50
  385.5 5.8 %cholesky.370 = f32[64,64]{1,0:T(8,128)S(1)} custom-call(f32[64,64]{1,0:T(8,128)S(1)} %fusion.29), custom_call_target="Cholesky" | custom-call | tf_op jit(solution)/shard_map/jit(cholesky)/cholesky | solution.py:16
  391.4 0.6 compare_reduce_fusion.5
  392.0 0.7 fusion.12
  392.7 4.9 %custom-call.40 = f32[1,64,64]{1,2,0:T(8,128)S(1)} custom-call(f32[1,64,64]{2,1,0:T(8,128)S(1)} %fusion.12), custom_call_target="InvertDiagBlocksLowerTriangular" | custom-call | tf_op jit(solution)/shard_map/triangular_solve/custom-call.8 | solution.py:17
  397.6 0.3 convolution_bitcast_fusion.6
  397.9 1.2 fusion.49
  399.1 0.9 fusion.48
  400.4 5.8 %cholesky.381 = f32[64,64]{1,0:T(8,128)S(1)} custom-call(f32[64,64]{1,0:T(8,128)S(1)} %fusion.27), custom_call_target="Cholesky" | custom-call | tf_op jit(solution)/shard_map/jit(cholesky)/cholesky | solution.py:16
  406.3 0.6 compare_reduce_fusion.4
  406.9 0.7 fusion.13
  407.6 4.9 %custom-call.41 = f32[1,64,64]{1,2,0:T(8,128)S(1)} custom-call(f32[1,64,64]{2,1,0:T(8,128)S(1)} %fusion.13), custom_call_target="InvertDiagBlocksLowerTriangular" | custom-call | tf_op jit(solution)/shard_map/triangular_solve/custom-call.8 | solution.py:17
  412.5 0.3 convolution_bitcast_fusion.5
  412.8 1.2 fusion.47
  414.0 0.9 fusion.46
  415.0 0.3 fusion.55
  415.3 5.8 %cholesky.392 = f32[64,64]{1,0:T(8,128)S(1)} custom-call(f32[64,64]{1,0:T(8,128)S(1)} %fusion.25), custom_call_target="Cholesky" | custom-call | tf_op jit(solution)/shard_map/jit(cholesky)/cholesky | solution.py:16
  421.2 0.6 compare_reduce_fusion.3
  421.9 0.7 fusion.14
  422.5 4.9 %custom-call.42 = f32[1,64,64]{1,2,0:T(8,128)S(1)} custom-call(f32[1,64,64]{2,1,0:T(8,128)S(1)} %fusion.14), custom_call_target="InvertDiagBlocksLowerTriangular" | custom-call | tf_op jit(solution)/shard_map/triangular_solve/custom-call.8 | solution.py:17
  427.4 0.5 convolution_bitcast_fusion.4
  427.9 1.2 fusion.45
  429.1 0.9 fusion.44
  430.1 0.3 fusion.56
  430.4 5.8 %cholesky.403 = f32[64,64]{1,0:T(8,128)S(1)} custom-call(f32[64,64]{1,0:T(8,128)S(1)} %fusion.23), custom_call_target="Cholesky" | custom-call | tf_op jit(solution)/shard_map/jit(cholesky)/cholesky | solution.py:16
  436.3 0.6 compare_reduce_fusion.2
  437.0 0.7 fusion.15
  437.6 4.9 %custom-call.43 = f32[1,64,64]{1,2,0:T(8,128)S(1)} custom-call(f32[1,64,64]{2,1,0:T(8,128)S(1)} %fusion.15), custom_call_target="InvertDiagBlocksLowerTriangular" | custom-call | tf_op jit(solution)/shard_map/triangular_solve/custom-call.8 | solution.py:17
  442.5 0.3 convolution_bitcast_fusion.3
  442.9 1.2 fusion.43
  444.1 0.9 fusion.42
  445.0 0.3 fusion.57
  445.4 5.8 %cholesky.414 = f32[64,64]{1,0:T(8,128)S(1)} custom-call(f32[64,64]{1,0:T(8,128)S(1)} %fusion.21), custom_call_target="Cholesky" | custom-call | tf_op jit(solution)/shard_map/jit(cholesky)/cholesky | solution.py:16
  451.2 0.6 compare_reduce_fusion.1
  451.9 0.7 fusion.16
  452.6 4.9 %custom-call.44 = f32[1,64,64]{1,2,0:T(8,128)S(1)} custom-call(f32[1,64,64]{2,1,0:T(8,128)S(1)} %fusion.16), custom_call_target="InvertDiagBlocksLowerTriangular" | custom-call | tf_op jit(solution)/shard_map/triangular_solve/custom-call.8 | solution.py:17
  457.4 0.3 convolution_bitcast_fusion.2
  457.8 1.2 fusion.41
  459.0 0.9 fusion.40
  460.3 5.8 %cholesky.425 = f32[64,64]{1,0:T(8,128)S(1)} custom-call(f32[64,64]{1,0:T(8,128)S(1)} %fusion.19), custom_call_target="Cholesky" | custom-call | tf_op jit(solution)/shard_map/jit(cholesky)/cholesky | solution.py:16
  466.2 0.6 compare_reduce_fusion
  466.8 0.7 fusion.17
  467.5 4.9 %custom-call.45 = f32[1,64,64]{1,2,0:T(8,128)S(1)} custom-call(f32[1,64,64]{2,1,0:T(8,128)S(1)} %fusion.17), custom_call_target="InvertDiagBlocksLowerTriangular" | custom-call | tf_op jit(solution)/shard_map/triangular_solve/custom-call.8 | solution.py:17
  472.4 0.5 convolution_bitcast_fusion.1
  472.9 7.0 %convolution_bitcast_fusion = f32[2048,64]{0,1:T(8,128)} fusion(f32[512,64]{0,1:T(8,128)S(1)} %convolution_bitcast_fusion.1, f32[2048,512]{1,0:T(8,128)} %param.5), kind=kOutput, calls=%fused_computation | convolution fusion | flops 805306368 | bytes 4849664 | tf_op jit(solution)/shard_map/dot_general | solution.py:33
  (35 shorter events, 2.2 us)
Async XLA Ops:
  6.5 376.0 %copy-start = (f32[512,64]{0,1:T(8,128)S(1)}, f32[512,64]{0,1:T(8,128)}, u32[]{:S(2)}) copy-start(f32[512,64]{0,1:T(8,128)} %param.6) | copy-start | bytes 393220
  6.5 289.7 %all-reduce.3.cloned.1.call-start = ((), (), s32[]{:S(2)}) async-start(), calls=%async_computation | async-start | bytes 2097152 | tf_op jit(solution)/shard_map/psum | solution.py:22
Sparse Core Ops, SparseCore 0:
  18.2 278.0 all-reduce.2
where the time goes:
time: 491 us; the launch traced here: 487 us
  waiting for transfers between devices  278 us (57%)
  other arithmetic  153 us (31%)
  matrix products  37.5 us (8%)
  between operations  16.6 us (3%)
    psum x1, waiting for transfers between devices, body(): gram = lax.psum(local_gram, ('raster', 'slit'))  278 us
    another operation x14, other arithmetic, body(): upper = jnp.linalg.cholesky(gram).T  78.6 us
    another operation x18, other arithmetic, orthonormal(): lower = jnp.linalg.cholesky(cross_of(image))  39.1 us
    another operation x12, other arithmetic, orthonormal(): lax.linalg.triangular_solve(lower, image, left_side=False, lower=True, tr...  33.3 us
    dot_general x7, matrix products, cross_of(): jnp.dot(matrix.T, matrix, precision=lax.Precision.HIGHEST, preferred_elem...  13 us
  transfers between devices with their start and end apart: 1, of which 1 were waited for; matrix products, arithmetic and copies ran while one was open for 0% of the time, Pallas kernels for 0%

commit v1 on v0

v1 whole, which is shorter than its diff:
```python
import functools

import jax
import jax.numpy as jnp
from jax import lax
from jax.experimental import pallas as pl
from jax.experimental.pallas import tpu as pltpu
from jax.sharding import Mesh, PartitionSpec as P

W = 512
K = 64
ITERS = 6
CHUNK = 256
HALF = 6 * 128
F32 = jnp.float32
BF16 = jnp.bfloat16
NN = (((1,), (0,)), ((), ()))
NT = (((1,), (1,)), ((), ()))
TN = (((0,), (0,)), ((), ()))


def mul(a, b, dims):
    return lax.dot_general(a, b, dims, preferred_element_type=F32)


def split(value):
    high = value.astype(BF16)
    return high, (value - high.astype(F32)).astype(BF16)


def gram_kernel(core_ref, spectra_ref, keep_ref, send_ref, acc):
    step = pl.program_id(0)

    @pl.when(step == 0)
    def _():
        acc[...] = jnp.zeros_like(acc)

    high, low = split(spectra_ref[...])
    h0, h1 = high[:, :256], high[:, 256:]
    l0, l1 = low[:, :256], low[:, 256:]
    acc[0] += 0.5 * mul(h0, h0, TN) + mul(h0, l0, TN)
    acc[1] += mul(h0, h1, TN) + mul(h0, l1, TN) + mul(l0, h1, TN)
    acc[2] += 0.5 * mul(h1, h1, TN) + mul(h1, l1, TN)

    @pl.when(step == pl.num_programs(0) - 1)
    def _():
        core = core_ref[0]
        for ref, half in ((keep_ref, core), (send_ref, 1 - core)):
            rows = pl.ds(pl.multiple_of(half * 128, 128), 128)
            for block in range(3):
                for side in range(2):
                    at = (2 * block + side) * 128
                    ref[at : at + 128, :] = acc[block, rows, side * 128 : side * 128 + 128]


def gram_halves(core, spectra):
    rows = spectra.shape[0]
    half = jax.ShapeDtypeStruct((HALF, 128), F32)
    whole = pl.BlockSpec((HALF, 128), lambda i: (0, 0))
    return pl.pallas_call(
        gram_kernel,
        grid=(rows // CHUNK,),
        in_specs=[
            pl.BlockSpec(memory_space=pltpu.SMEM),
            pl.BlockSpec((CHUNK, W), lambda i: (i, 0)),
        ],
        out_specs=[whole, whole],
        out_shape=[half, half],
        scratch_shapes=[pltpu.VMEM((3, 256, 256), F32)],
        compiler_params=pltpu.CompilerParams(vmem_limit_bytes=32 * 1024 * 1024),
    )(core, spectra)


def splat(value, i, j):
    return jnp.broadcast_to(value[i : i + 1, j : j + 1], (8, 128))


def eliminate(a, out_ref):
    for b in range(8):
        pivot = a[b]
        lane = 64 + 8 * b
        d = {(i, j): splat(pivot, i, lane + j) for i in range(8) for j in range(i + 1)}
        inv = []
        x = {}
        for k in range(8):
            inv.append(1.0 / d[k, k])
            m = {i: d[i, k] * inv[k] for i in range(k + 1, 8)}
            for i in range(k + 1, 8):
                for j in range(k + 1, i + 1):
                    d[i, j] = d[i, j] - (d[i, k] * d[j, k]) * inv[k]
                for j in range(k):
                    x[i, j] = x[i, j] - m[i] * x[k, j]
                x[i, k] = -m[i]
        rows = [jnp.broadcast_to(pivot[j : j + 1, :], (8, 128)) for j in range(8)]
        new = []
        for r in range(8):
            total = rows[r]
            for j in range(r):
                total = total + x[r, j] * rows[j]
            new.append(total)
        for r in range(8):
            out_ref[8 * b + r : 8 * b + r + 1, :] = (new[r] * lax.rsqrt(d[r, r]))[0:1, :]
        if b == 7:
            break
        scaled = [new[r] * inv[r] for r in range(8)]
        q = []
        for c in range(8):
            total = scaled[c]
            for j in range(c + 1, 8):
                total = total + x[j, c] * scaled[j]
            q.append(total)
        for i in range(b + 1, 8):
            total = a[i]
            for c in range(8):
                total = total - jnp.broadcast_to(a[i][:, lane + c : lane + c + 1], (8, 128)) * q[c]
            a[i] = total


def iterate_kernel(core_ref, mine_ref, other_ref, start_ref, spectra_ref, out_ref, gh, gl, basis, rp, sbuf, obuf, sem, osem):
    load = pltpu.make_async_copy(spectra_ref, sbuf, sem)
    load.start()
    core = core_ref[0]
    zero_is_mine = core == 0

    def half(h, block):
        at = slice(block * 128, block * 128 + 128)
        a, b = mine_ref[at, :], other_ref[at, :]
        return jnp.where(zero_is_mine, a, b) if h == 0 else jnp.where(zero_is_mine, b, a)

    def whole(block):
        return jnp.concatenate(
            [jnp.concatenate([half(h, 2 * block), half(h, 2 * block + 1)], axis=1) for h in range(2)], axis=0
        )

    def put(i, j, value):
        at = (slice(256 * i, 256 * i + 256), slice(256 * j, 256 * j + 256))
        gh[at], gl[at] = split(value * 2.0**-20)

    t0, t1, t2 = whole(0), whole(1), whole(2)
    put(0, 0, t0 + t0.T)
    put(0, 1, t1)
    put(1, 0, t1.T)
    put(1, 1, t2 + t2.T)

    basis[...] = start_ref[...].T
    lanes = lax.broadcasted_iota(jnp.int32, (K, 128), 1)
    eye = (lanes == lax.broadcasted_iota(jnp.int32, (K, 128), 0)).astype(F32)

    def step(_, carry):
        bh, bl = split(basis[...])
        both = mul(jnp.concatenate([bh, bl], axis=0), gh[...], NN)
        image = both[:K] + both[K:] + mul(bh, gl[...], NN)
        ih, il = split(image)
        first = mul(jnp.concatenate([ih, il], axis=0), jnp.concatenate([il, ih], axis=0), NT)
        cross = first[:K] + first[K:] + mul(ih, jnp.concatenate([ih, il], axis=0), NT)
        a = jnp.where(lanes < K, eye, cross)
        eliminate([a[8 * i : 8 * i + 8, :] for i in range(8)], rp)
        xh, xl = split(rp[:, :K])
        both = mul(jnp.concatenate([xh, xl], axis=0), ih, NN)
        basis[...] = both[:K] + both[K:] + mul(xh, il, NN)
        return carry

    lax.fori_loop(0, ITERS, step, 0)
    bh, bl = split(basis[...])
    load.wait()
    rows = 512
    both = jnp.concatenate([bh, bl], axis=0)

    @pl.loop(0, sbuf.shape[0] // rows)
    def _(i):
        at = pl.ds(pl.multiple_of(i * rows, rows), rows)
        sh, sl = split(sbuf[at, :])
        wide = mul(sh, both, NT)
        obuf[at, :] = wide[:, :K] + wide[:, K:] + mul(sl, bh, NT)

    store = pltpu.make_async_copy(obuf, out_ref, osem)
    store.start()
    store.wait()


def finish(core, mine, other, start, spectra):
    rows = spectra.shape[0]
    vmem = pl.BlockSpec(memory_space=pltpu.VMEM)
    hbm = pl.BlockSpec(memory_space=pl.ANY)
    return pl.pallas_call(
        iterate_kernel,
        in_specs=[pl.BlockSpec(memory_space=pltpu.SMEM), vmem, vmem, vmem, hbm],
        out_specs=hbm,
        out_shape=jax.ShapeDtypeStruct((rows, K), F32),
        scratch_shapes=[
            pltpu.VMEM((W, W), BF16),
            pltpu.VMEM((W, W), BF16),
            pltpu.VMEM((K, W), F32),
            pltpu.VMEM((K, 128), F32),
            pltpu.VMEM((rows, W), F32),
            pltpu.VMEM((rows, K), F32),
            pltpu.SemaphoreType.DMA,
            pltpu.SemaphoreType.DMA,
        ],
        compiler_params=pltpu.CompilerParams(vmem_limit_bytes=48 * 1024 * 1024),
    )(core, mine, other, start, spectra)


def swap(value):
    return lax.ppermute(value, "core", [(0, 1), (1, 0)])


def spread(piece, axis, copies):
    return lax.all_to_all(jnp.broadcast_to(piece[None], (copies, *piece.shape)), axis, 0, 0)


def body(raster, z, spectra, start):
    core = lax.axis_index("core").astype(jnp.int32).reshape(1)
    keep, send = gram_halves(core, spectra)
    part = keep + swap(send)
    part = lax.all_to_all(part.reshape(raster, HALF // raster, 128), "raster", 0, 0)
    piece = jnp.sum(part, axis=0)
    piece = jnp.sum(spread(piece, "z", z), axis=0)
    mine = spread(piece, "raster", raster).reshape(HALF, 128)
    return finish(core, mine, swap(mine), start, spectra)


def solution(mesh):
    raster, slit = mesh.devices.shape
    inner = Mesh(mesh.devices.reshape(raster, slit // 2, 2), ("raster", "z", "core"))
    rows = P(("raster", "z", "core"), None)
    return jax.shard_map(
        functools.partial(body, raster, slit // 2),
        mesh=inner,
        in_specs=(rows, P()),
        out_specs=rows,
        check_vma=False,
    )
```

time: 491 us -> 96.8 us (0.20)
  waiting for transfers between devices: 278 us -> 2.52 us
  other arithmetic: 153 us -> 0.09 us
  blocking collectives: 0 us -> 51 us
  matrix products: 37.5 us -> 0 us
  Pallas kernels: 0 us -> 23.4 us
  between operations: 16.6 us -> 0.08 us
  starting transfers between devices: 0.01 us -> 15.9 us
    psum x1 -> x0, waiting for transfers between devices: 278 us -> none  [body(): gram = lax.psum(local_gram, ('raster', 'slit'))]
    another operation x44 -> x0, other arithmetic: 151 us -> none  [the longest x14 78.6 us: body(): upper = jnp.linalg.cholesky(gram).T]
    all_to_all x0 -> x3, blocking collectives: none -> 51 us  [the longest x2 35.1 us: spread(): lax.all_to_all(jnp.broadcast_to(piece[None], (copies, *piece.shape)), axi...]
    dot_general x20 -> x0, matrix products: 33.3 us -> none  [the longest x7 13 us: cross_of(): jnp.dot(matrix.T, matrix, precision=lax.Precision.HIGHEST, preferred_elem...]
    pallas_call x0 -> x2, Pallas kernels: none -> 23.4 us  [the longest x1 19.6 us: finish(): pl.pallas_call(iterate_kernel, in_specs=[pl.BlockSpec(memory_space=pltpu....]
    ppermute x0 -> x2, starting transfers between devices: none -> 15.9 us  [swap(): return lax.ppermute(value, 'core', [(0, 1), (1, 0)])]
  transfers between devices with their start and end apart: 1 -> 2, of which waited for: 1 -> 2; matrix products, arithmetic and copies ran while one was open for 0% -> 0% of each run, Pallas kernels for 0% -> 0%
where the time goes in v1:
time: 96.8 us; the launch traced here: 96.5 us
  blocking collectives  51 us (53%)
  Pallas kernels  23.4 us (24%)
  starting transfers between devices  15.9 us (16%)
  local copies, waits for them, and re-layouts  3.46 us (4%)
  waiting for transfers between devices  2.52 us (3%)
    all_to_all x2, blocking collectives, spread(): lax.all_to_all(jnp.broadcast_to(piece[None], (copies, *piece.shape)), axi...  35.1 us
    pallas_call x1, Pallas kernels, finish(): pl.pallas_call(iterate_kernel, in_specs=[pl.BlockSpec(memory_space=pltpu....  19.6 us
    ppermute x2, starting transfers between devices, swap(): return lax.ppermute(value, 'core', [(0, 1), (1, 0)])  15.9 us
    all_to_all x1, blocking collectives, body(): lax.all_to_all(part.reshape(raster, HALF // raster, 128), 'raster', 0, 0)  15.9 us
    pallas_call x1, Pallas kernels, gram_halves(): pl.pallas_call(gram_kernel, grid=(rows // CHUNK,), in_specs=[pl.BlockSpec...  3.74 us
    ppermute x2, waiting for transfers between devices, swap(): return lax.ppermute(value, 'core', [(0, 1), (1, 0)])  2.52 us
    unnamed x5, local copies, waits for them, and re-layouts  2.31 us
  transfers between devices with their start and end apart: 2, of which 2 were waited for; matrix products, arithmetic and copies ran while one was open for 0% of the time, Pallas kernels for 0%

profile of v1, /device:TPU:1, one launch (start us, length us, event | category | flops | bytes accessed | tf_op | source)
XLA Modules:
  0.0 96.5 jit_solution(13355465886073515289)
XLA Ops:
  0.0 0.0 copy-start
  0.0 2.2 %copy-done = f32[2048,512]{1,0:T(8,128)S(1)} copy-done((f32[2048,512]{1,0:T(8,128)S(1)}, f32[2048,512]{1,0:T(8,128)}, u32[]{:S(2)}) %copy-start) | copy-done | bytes 4194328
  2.2 0.0 copy-start.1
  2.2 3.7 %shard_map.28 = (f32[768,128]{1,0:T(8,128)S(1)}, f32[768,128]{1,0:T(8,128)S(1)}) custom-call(s32[1]{0:T(128)} %bitcast.core_ref, f32[2048,512]{1,0:T(8,128)S(1)} %copy-done), custom_call_target="tpu_custom_call" | custom-call | tf_op jit(solution)/shard_map/pallas_call | solution.py:60
  5.9 8.8 %collective-permute-start = (f32[768,128]{1,0:T(8,128)S(1)}, f32[768,128]{1,0:T(8,128)S(1)}, u32[]{:S(2)}, u32[]{:S(2)}) collective-permute-start(f32[768,128]{1,0:T(8,128)S(1)} %get-tuple-element.8), channel_id=1, source_target_pairs={{0,1},{1,0},{2,3},{3,2},{4,5},{5,4},{6,7},{7,6},{8,9},{9,8},{10,11... | collective-permute-start | bytes 1179656 | tf_op jit(solution)/shard_map/ppermute | solution.py:205
  14.7 1.3 %collective-permute-done = f32[768,128]{1,0:T(8,128)S(1)} collective-permute-done((f32[768,128]{1,0:T(8,128)S(1)}, f32[768,128]{1,0:T(8,128)S(1)}, u32[]{:S(2)}, u32[]{:S(2)}) %collective-permute-start) | collective-permute-done | bytes 393248 | tf_op jit(solution)/shard_map/ppermute | solution.py:205
  16.1 15.9 %all_to_all.15 = f32[32,24,128]{2,1,0:T(8,128)S(1)} all-to-all(f32[32,24,128]{2,1,0:T(8,128)S(1)} %bitcast.5), channel_id=1, replica_groups=mesh['raster'=32,'z'=8,'core'=2] {'raster'}, dimensions={0} | all-to-all | bytes 786432 | tf_op jit(solution)/shard_map/all_to_all | solution.py:216
  32.0 17.4 %all_to_all.16 = f32[8,24,128]{2,1,0:T(8,128)S(1)} all-to-all(f32[8,24,128]{2,1,0:T(8,128)S(1)} %broadcast_in_dim.4), channel_id=1, replica_groups=mesh['raster'=32,'z'=8,'core'=2] {'z'}, dimensions={0} | all-to-all | bytes 196608 | tf_op jit(solution)/shard_map/all_to_all | solution.py:209
  49.5 17.7 %all_to_all.17 = f32[32,24,128]{2,1,0:T(8,128)S(1)} all-to-all(f32[32,24,128]{2,1,0:T(8,128)S(1)} %broadcast_in_dim.5), channel_id=1, replica_groups=mesh['raster'=32,'z'=8,'core'=2] {'raster'}, dimensions={0} | all-to-all | bytes 786432 | tf_op jit(solution)/shard_map/all_to_all | solution.py:209
  67.2 7.2 %collective-permute-start.1 = (f32[768,128]{1,0:T(8,128)S(1)}, f32[768,128]{1,0:T(8,128)S(1)}, u32[]{:S(2)}, u32[]{:S(2)}) collective-permute-start(f32[768,128]{1,0:T(8,128)S(1)} %bitcast.3), channel_id=1, source_target_pairs={{0,1},{1,0},{2,3},{3,2},{4,5},{5,4},{6,7},{7,6},{8,9},{9,8},{10,11... | collective-permute-start | bytes 1179656 | tf_op jit(solution)/shard_map/ppermute | solution.py:205
  74.4 0.0 copy-done.1
  74.4 0.1 copy.5.start_ref
  74.5 1.2 %collective-permute-done.1.other_ref = f32[768,128]{1,0:T(8,128)S(1)} collective-permute-done((f32[768,128]{1,0:T(8,128)S(1)}, f32[768,128]{1,0:T(8,128)S(1)}, u32[]{:S(2)}, u32[]{:S(2)}) %collective-permute-start.1) | collective-permute-done | bytes 393248 | tf_op jit(solution)/shard_map/ppermute | solution.py:205
  75.7 19.6 %shard_map.29 = f32[2048,64]{1,0:T(8,128)S(1)} custom-call(s32[1]{0:T(128)} %bitcast.core_ref, f32[768,128]{1,0:T(8,128)S(1)} %bitcast.4, f32[768,128]{1,0:T(8,128)S(1)} %collective-permute-done.1.other_ref, f32[512,64]{1,0:T(8,128)S(1)} %copy.5.start_ref, f32[2048,512]{1,0:T(8,128)} %spectra_ref.3), custom_call_target="tpu_custom_call" | custom-call | tf_op jit(solution)/shard_map/pallas_call | solution.py:185
  95.4 1.1 %copy.6 = f32[2048,64]{0,1:T(8,128)} copy(f32[2048,64]{1,0:T(8,128)S(1)} %shard_map.29) | data formatting | bytes 1048576 | tf_op jit(solution)/shard_map/pallas_call | solution.py:185
  (5 shorter events, 0.1 us)
Async XLA Ops:
  0.0 2.2 %copy-start = (f32[2048,512]{1,0:T(8,128)S(1)}, f32[2048,512]{1,0:T(8,128)}, u32[]{:S(2)}) copy-start(f32[2048,512]{1,0:T(8,128)} %spectra_ref.3) | copy-start | bytes 12582916
  2.2 72.2 %copy-start.1 = (f32[512,64]{0,1:T(8,128)S(1)}, f32[512,64]{0,1:T(8,128)}, u32[]{:S(2)}) copy-start(f32[512,64]{0,1:T(8,128)} %param.3) | copy-start | bytes 393220
  5.9 10.1 %collective-permute-start = (f32[768,128]{1,0:T(8,128)S(1)}, f32[768,128]{1,0:T(8,128)S(1)}, u32[]{:S(2)}, u32[]{:S(2)}) collective-permute-start(f32[768,128]{1,0:T(8,128)S(1)} %get-tuple-element.8), channel_id=1, source_target_pairs={{0,1},{1,0},{2,3},{3,2},{4,5},{5,4},{6,7},{7,6},{8,9},{9,8},{10,11... | collective-permute-start | bytes 1179656 | tf_op jit(solution)/shard_map/ppermute | solution.py:205
  67.2 8.5 %collective-permute-start.1 = (f32[768,128]{1,0:T(8,128)S(1)}, f32[768,128]{1,0:T(8,128)S(1)}, u32[]{:S(2)}, u32[]{:S(2)}) collective-permute-start(f32[768,128]{1,0:T(8,128)S(1)} %bitcast.3), channel_id=1, source_target_pairs={{0,1},{1,0},{2,3},{3,2},{4,5},{5,4},{6,7},{7,6},{8,9},{9,8},{10,11... | collective-permute-start | bytes 1179656 | tf_op jit(solution)/shard_map/ppermute | solution.py:205

commit v2 on v1

v2 whole, which is shorter than its diff:
```python
import functools

import jax
import jax.numpy as jnp
from jax import lax
from jax.experimental import pallas as pl
from jax.experimental.pallas import tpu as pltpu
from jax.sharding import Mesh, PartitionSpec as P

W = 512
K = 64
ITERS = 6
CHUNK = 512
HALF = 6 * 128
F32 = jnp.float32
BF16 = jnp.bfloat16
NN = (((1,), (0,)), ((), ()))
NT = (((1,), (1,)), ((), ()))
TN = (((0,), (0,)), ((), ()))


def mul(a, b, dims):
    return lax.dot_general(a, b, dims, preferred_element_type=F32)


def split(value):
    high = value.astype(BF16)
    return high, (value - high.astype(F32)).astype(BF16)


def gram_kernel(core_ref, spectra_ref, keep_ref, send_ref, buf, acc, sems):
    parts = buf.shape[0] // CHUNK
    loads = []
    for i in range(parts):
        at = slice(i * CHUNK, i * CHUNK + CHUNK)
        loads.append(pltpu.make_async_copy(spectra_ref.at[at], buf.at[at], sems.at[i]))
        loads[-1].start()
    for i in range(parts):
        loads[i].wait()
        high, low = split(buf[i * CHUNK : i * CHUNK + CHUNK, :])
        h0, h1 = high[:, :256], high[:, 256:]
        l0, l1 = low[:, :256], low[:, 256:]
        sums = (
            0.5 * mul(h0, h0, TN) + mul(h0, l0, TN),
            mul(h0, h1, TN) + mul(h0, l1, TN) + mul(l0, h1, TN),
            0.5 * mul(h1, h1, TN) + mul(h1, l1, TN),
        )
        for block in range(3):
            acc[block] = acc[block] + sums[block] if i else sums[block]
    for ref, half in ((keep_ref, core_ref[0]), (send_ref, 1 - core_ref[0])):
        rows = pl.ds(pl.multiple_of(half * 128, 128), 128)
        for block in range(3):
            for side in range(2):
                at = (2 * block + side) * 128
                ref[at : at + 128, :] = acc[block, rows, side * 128 : side * 128 + 128]


def gram_halves(core, spectra):
    rows = spectra.shape[0]
    half = jax.ShapeDtypeStruct((HALF, 128), F32)
    vmem = pl.BlockSpec(memory_space=pltpu.VMEM)
    return pl.pallas_call(
        gram_kernel,
        in_specs=[pl.BlockSpec(memory_space=pltpu.SMEM), pl.BlockSpec(memory_space=pl.ANY)],
        out_specs=[vmem, vmem],
        out_shape=[half, half],
        scratch_shapes=[
            pltpu.VMEM((rows, W), F32),
            pltpu.VMEM((3, 256, 256), F32),
            pltpu.SemaphoreType.DMA((rows // CHUNK,)),
        ],
        compiler_params=pltpu.CompilerParams(vmem_limit_bytes=52 * 1024 * 1024),
    )(core, spectra)


def tree(terms):
    while len(terms) > 1:
        terms = [terms[i] + terms[i + 1] if i + 1 < len(terms) else terms[i] for i in range(0, len(terms), 2)]
    return terms[0]


def lanes_of(group, lane):
    return jnp.broadcast_to(group[:, lane : lane + 1], (8, 128))


def row_of(group, i):
    return jnp.broadcast_to(group[i : i + 1, :], (8, 128))


def eliminate(a, out_ref):
    sub = lax.broadcasted_iota(jnp.int32, (8, 128), 0)
    square = [lanes_of(a[0], 64 + j) for j in range(8)]
    for b in range(8):
        lane = 64 + 8 * b
        nearest = [lanes_of(a[b + 1], lane + j) for j in range(8)] if b < 7 else []
        following = [lanes_of(a[b + 1], lane + 8 + j) for j in range(8)] if b < 7 else []
        rows = a[b]
        scaled = []
        inverse = jnp.zeros((8, 128), F32)
        for k in range(8):
            s = {c: row_of(square[k], c) for c in range(k, 8)}
            inv = pl.reciprocal(s[k], approx=True)
            below = jnp.where(sub > k, square[k], 0.0)
            down = below * inv
            for c in range(k + 1, 8):
                square[c] = square[c] - ((below * s[c]) * inv if c == k + 1 else down * s[c])
            row = row_of(rows, k)
            rows = rows - down * row
            inverse = jnp.where(sub == k, inv, inverse)
            if b < 7:
                scaled.append(row * inv)
                down = nearest[k] * inv
                for c in range(k + 1, 8):
                    nearest[c] = nearest[c] - down * s[c]
                for c in range(8):
                    following[c] = following[c] - down * row_of(nearest[k], c)
        out_ref[8 * b : 8 * b + 8, :] = rows * (inverse * lax.rsqrt(inverse))
        if b == 7:
            break
        a[b + 1] = a[b + 1] - tree([nearest[k] * scaled[k] for k in range(8)])
        panels = {i: [lanes_of(a[i], lane + j) for j in range(8)] for i in range(b + 2, 8)}
        if panels:
            q = rows * inverse
            for k in range(7, 0, -1):
                q = q - jnp.where(sub < k, square[k] * inverse, 0.0) * row_of(q, k)
            q = [row_of(q, c) for c in range(8)]
            for i, panel in panels.items():
                a[i] = a[i] - tree([panel[c] * q[c] for c in range(8)])
        square = following


def iterate_kernel(core_ref, mine_ref, other_ref, start_ref, spectra_ref, out_ref, gh, gl, basis, rp, sbuf, obuf, sem, osem):
    load = pltpu.make_async_copy(spectra_ref, sbuf, sem)
    load.start()
    core = core_ref[0]
    zero_is_mine = core == 0

    def half(h, block):
        at = slice(block * 128, block * 128 + 128)
        a, b = mine_ref[at, :], other_ref[at, :]
        return jnp.where(zero_is_mine, a, b) if h == 0 else jnp.where(zero_is_mine, b, a)

    def whole(block):
        return jnp.concatenate(
            [jnp.concatenate([half(h, 2 * block), half(h, 2 * block + 1)], axis=1) for h in range(2)], axis=0
        )

    def put(i, j, value):
        at = (slice(256 * i, 256 * i + 256), slice(256 * j, 256 * j + 256))
        gh[at], gl[at] = split(value * 2.0**-20)

    t0, t1, t2 = whole(0), whole(1), whole(2)
    put(0, 0, t0 + t0.T)
    put(0, 1, t1)
    put(1, 0, t1.T)
    put(1, 1, t2 + t2.T)

    basis[...] = start_ref[...]
    lanes = lax.broadcasted_iota(jnp.int32, (K, 128), 1)
    eye = (lanes == lax.broadcasted_iota(jnp.int32, (K, 128), 0)).astype(F32)

    def step(_, carry):
        bh, bl = split(basis[...])
        both = mul(jnp.concatenate([bh, bl], axis=0), gh[...], NN)
        image = both[:K] + both[K:] + mul(bh, gl[...], NN)
        ih, il = split(image)
        first = mul(jnp.concatenate([ih, il], axis=0), jnp.concatenate([il, ih], axis=0), NT)
        cross = first[:K] + first[K:] + mul(ih, jnp.concatenate([ih, il], axis=0), NT)
        a = jnp.where(lanes < K, eye, cross)
        eliminate([a[8 * i : 8 * i + 8, :] for i in range(8)], rp)
        xh, xl = split(rp[:, :K])
        both = mul(jnp.concatenate([xh, xl], axis=0), ih, NN)
        basis[...] = both[:K] + both[K:] + mul(xh, il, NN)
        return carry

    lax.fori_loop(0, ITERS, step, 0)
    bh, bl = split(basis[...])
    load.wait()
    both = jnp.concatenate([bh, bl], axis=0)
    rows = 512
    stores = []
    for i in range(sbuf.shape[0] // rows):
        at = slice(i * rows, i * rows + rows)
        sh, sl = split(sbuf[at, :])
        wide = mul(both, sh, NT)
        obuf[:, at] = wide[:K] + wide[K:] + mul(bh, sl, NT)
        stores.append(pltpu.make_async_copy(obuf.at[:, at], out_ref.at[:, at], osem.at[i]))
        stores[-1].start()
    for store in stores:
        store.wait()


def finish(core, mine, other, start, spectra):
    rows = spectra.shape[0]
    vmem = pl.BlockSpec(memory_space=pltpu.VMEM)
    hbm = pl.BlockSpec(memory_space=pl.ANY)
    return pl.pallas_call(
        iterate_kernel,
        in_specs=[pl.BlockSpec(memory_space=pltpu.SMEM), vmem, vmem, vmem, hbm],
        out_specs=hbm,
        out_shape=jax.ShapeDtypeStruct((K, rows), F32),
        scratch_shapes=[
            pltpu.VMEM((W, W), BF16),
            pltpu.VMEM((W, W), BF16),
            pltpu.VMEM((K, W), F32),
            pltpu.VMEM((K, 128), F32),
            pltpu.VMEM((rows, W), F32),
            pltpu.VMEM((K, rows), F32),
            pltpu.SemaphoreType.DMA,
            pltpu.SemaphoreType.DMA((rows // 512,)),
        ],
        compiler_params=pltpu.CompilerParams(vmem_limit_bytes=52 * 1024 * 1024),
    )(core, mine, other, start, spectra)


def swap(value):
    return lax.ppermute(value, "core", [(0, 1), (1, 0)])


def spread(piece, axis, copies):
    return lax.all_to_all(jnp.broadcast_to(piece[None], (copies, *piece.shape)), axis, 0, 0)


def body(raster, z, spectra, start):
    core = lax.axis_index("core").astype(jnp.int32).reshape(1)
    keep, send = gram_halves(core, spectra)
    part = keep + swap(send)
    part = lax.all_to_all(part.reshape(raster, HALF // raster, 128), "raster", 0, 0)
    piece = jnp.sum(part, axis=0)
    piece = jnp.sum(spread(piece, "z", z), axis=0)
    mine = spread(piece, "raster", raster).reshape(HALF, 128)
    return finish(core, mine, swap(mine), start.T, spectra).T


def solution(mesh):
    raster, slit = mesh.devices.shape
    inner = Mesh(mesh.devices.reshape(raster, slit // 2, 2), ("raster", "z", "core"))
    rows = P(("raster", "z", "core"), None)
    return jax.shard_map(
        functools.partial(body, raster, slit // 2),
        mesh=inner,
        in_specs=(rows, P()),
        out_specs=rows,
        check_vma=False,
    )
```

time: 96.8 us -> 89 us (0.919)
  Pallas kernels: 23.4 us -> 18.9 us
  local copies, waits for them, and re-layouts: 3.46 us -> 0.04 us
    pallas_call x1, Pallas kernels: 19.6 us -> 14.9 us  [finish(): pl.pallas_call(iterate_kernel, in_specs=[pl.BlockSpec(memory_space=pltpu....]
    unnamed x5 -> x2, local copies, waits for them, and re-layouts: 2.31 us -> 0.01 us
    pallas_call x1 -> x0, local copies, waits for them, and re-layouts: 1.11 us -> none  [finish(): pl.pallas_call(iterate_kernel, in_specs=[pl.BlockSpec(memory_space=pltpu....]
where the time goes in v2:
time: 89 us; the launch traced here: 88.7 us
  blocking collectives  51 us (57%)
  Pallas kernels  18.9 us (21%)
  starting transfers between devices  15.9 us (18%)
  waiting for transfers between devices  2.65 us (3%)
    all_to_all x2, blocking collectives, spread(): lax.all_to_all(jnp.broadcast_to(piece[None], (copies, *piece.shape)), axi...  35.1 us
    ppermute x2, starting transfers between devices, swap(): return lax.ppermute(value, 'core', [(0, 1), (1, 0)])  15.9 us
    all_to_all x1, blocking collectives, body(): lax.all_to_all(part.reshape(raster, HALF // raster, 128), 'raster', 0, 0)  15.9 us
    pallas_call x1, Pallas kernels, finish(): pl.pallas_call(iterate_kernel, in_specs=[pl.BlockSpec(memory_space=pltpu....  14.9 us
    pallas_call x1, Pallas kernels, gram_halves(): pl.pallas_call(gram_kernel, in_specs=[pl.BlockSpec(memory_space=pltpu.SME...  4.02 us
    ppermute x2, waiting for transfers between devices, swap(): return lax.ppermute(value, 'core', [(0, 1), (1, 0)])  2.65 us
  transfers between devices with their start and end apart: 2, of which 2 were waited for; matrix products, arithmetic and copies ran while one was open for 0% of the time, Pallas kernels for 0%

profile of v2, /device:TPU:1, one launch (start us, length us, event | category | flops | bytes accessed | tf_op | source)
XLA Modules:
  0.0 88.7 jit_solution(16166531908301656448)
XLA Ops:
  0.0 0.0 copy-start
  0.0 4.0 %shard_map.28 = (f32[768,128]{1,0:T(8,128)S(1)}, f32[768,128]{1,0:T(8,128)S(1)}) custom-call(s32[1]{0:T(128)} %bitcast.core_ref, f32[2048,512]{1,0:T(8,128)} %spectra_ref.3), custom_call_target="tpu_custom_call" | custom-call | tf_op jit(solution)/shard_map/pallas_call | solution.py:62
  4.0 8.8 %collective-permute-start = (f32[768,128]{1,0:T(8,128)S(1)}, f32[768,128]{1,0:T(8,128)S(1)}, u32[]{:S(2)}, u32[]{:S(2)}) collective-permute-start(f32[768,128]{1,0:T(8,128)S(1)} %get-tuple-element.8), channel_id=1, source_target_pairs={{0,1},{1,0},{2,3},{3,2},{4,5},{5,4},{6,7},{7,6},{8,9},{9,8},{10,11... | collective-permute-start | bytes 1179656 | tf_op jit(solution)/shard_map/ppermute | solution.py:217
  12.8 1.3 %collective-permute-done = f32[768,128]{1,0:T(8,128)S(1)} collective-permute-done((f32[768,128]{1,0:T(8,128)S(1)}, f32[768,128]{1,0:T(8,128)S(1)}, u32[]{:S(2)}, u32[]{:S(2)}) %collective-permute-start) | collective-permute-done | bytes 393248 | tf_op jit(solution)/shard_map/ppermute | solution.py:217
  14.2 15.9 %all_to_all.15 = f32[32,24,128]{2,1,0:T(8,128)S(1)} all-to-all(f32[32,24,128]{2,1,0:T(8,128)S(1)} %bitcast.8), channel_id=1, replica_groups=mesh['raster'=32,'z'=8,'core'=2] {'raster'}, dimensions={0} | all-to-all | bytes 786432 | tf_op jit(solution)/shard_map/all_to_all | solution.py:228
  30.1 17.4 %all_to_all.16 = f32[8,24,128]{2,1,0:T(8,128)S(1)} all-to-all(f32[8,24,128]{2,1,0:T(8,128)S(1)} %broadcast_in_dim.4), channel_id=1, replica_groups=mesh['raster'=32,'z'=8,'core'=2] {'z'}, dimensions={0} | all-to-all | bytes 196608 | tf_op jit(solution)/shard_map/all_to_all | solution.py:221
  47.6 17.7 %all_to_all.17 = f32[32,24,128]{2,1,0:T(8,128)S(1)} all-to-all(f32[32,24,128]{2,1,0:T(8,128)S(1)} %broadcast_in_dim.5), channel_id=1, replica_groups=mesh['raster'=32,'z'=8,'core'=2] {'raster'}, dimensions={0} | all-to-all | bytes 786432 | tf_op jit(solution)/shard_map/all_to_all | solution.py:221
  65.3 7.2 %collective-permute-start.1 = (f32[768,128]{1,0:T(8,128)S(1)}, f32[768,128]{1,0:T(8,128)S(1)}, u32[]{:S(2)}, u32[]{:S(2)}) collective-permute-start(f32[768,128]{1,0:T(8,128)S(1)} %bitcast.5), channel_id=1, source_target_pairs={{0,1},{1,0},{2,3},{3,2},{4,5},{5,4},{6,7},{7,6},{8,9},{9,8},{10,11... | collective-permute-start | bytes 1179656 | tf_op jit(solution)/shard_map/ppermute | solution.py:217
  72.5 1.3 %collective-permute-done.1.other_ref = f32[768,128]{1,0:T(8,128)S(1)} collective-permute-done((f32[768,128]{1,0:T(8,128)S(1)}, f32[768,128]{1,0:T(8,128)S(1)}, u32[]{:S(2)}, u32[]{:S(2)}) %collective-permute-start.1) | collective-permute-done | bytes 393248 | tf_op jit(solution)/shard_map/ppermute | solution.py:217
  73.8 0.0 copy-done
  73.8 14.9 %shard_map.29 = f32[64,2048]{1,0:T(8,128)} custom-call(s32[1]{0:T(128)} %bitcast.core_ref, f32[768,128]{1,0:T(8,128)S(1)} %bitcast.6, f32[768,128]{1,0:T(8,128)S(1)} %collective-permute-done.1.other_ref, f32[64,512]{1,0:T(8,128)S(1)} %bitcast.7, f32[2048,512]{1,0:T(8,128)} %spectra_ref.3), custom_call_target="tpu_custom_call" | custom-call | tf_op jit(solution)/shard_map/pallas_call | solution.py:197
  (5 shorter events, 0.1 us)
Async XLA Ops:
  0.0 73.8 %copy-start = (f32[512,64]{0,1:T(8,128)S(1)}, f32[512,64]{0,1:T(8,128)}, u32[]{:S(2)}) copy-start(f32[512,64]{0,1:T(8,128)} %param.3) | copy-start | bytes 393220
  4.0 10.1 %collective-permute-start = (f32[768,128]{1,0:T(8,128)S(1)}, f32[768,128]{1,0:T(8,128)S(1)}, u32[]{:S(2)}, u32[]{:S(2)}) collective-permute-start(f32[768,128]{1,0:T(8,128)S(1)} %get-tuple-element.8), channel_id=1, source_target_pairs={{0,1},{1,0},{2,3},{3,2},{4,5},{5,4},{6,7},{7,6},{8,9},{9,8},{10,11... | collective-permute-start | bytes 1179656 | tf_op jit(solution)/shard_map/ppermute | solution.py:217
  65.3 8.5 %collective-permute-start.1 = (f32[768,128]{1,0:T(8,128)S(1)}, f32[768,128]{1,0:T(8,128)S(1)}, u32[]{:S(2)}, u32[]{:S(2)}) collective-permute-start(f32[768,128]{1,0:T(8,128)S(1)} %bitcast.5), channel_id=1, source_target_pairs={{0,1},{1,0},{2,3},{3,2},{4,5},{5,4},{6,7},{7,6},{8,9},{9,8},{10,11... | collective-permute-start | bytes 1179656 | tf_op jit(solution)/shard_map/ppermute | solution.py:217

commit v3 on v2

--- a/solution.py
+++ b/solution.py
@@ -11,7 +11,8 @@
 K = 64
 ITERS = 6
 CHUNK = 512
-HALF = 6 * 128
+HALF = 5 * 128
+BLOCKS = (((0, 0), (0, 1), (0, 2), (0, 3), (3, 3)), ((1, 1), (1, 2), (1, 3), (2, 2), (2, 3)))
 F32 = jnp.float32
 BF16 = jnp.bfloat16
 NN = (((1,), (0,)), ((), ()))
@@ -47,12 +48,24 @@
         )
         for block in range(3):
             acc[block] = acc[block] + sums[block] if i else sums[block]
-    for ref, half in ((keep_ref, core_ref[0]), (send_ref, 1 - core_ref[0])):
-        rows = pl.ds(pl.multiple_of(half * 128, 128), 128)
-        for block in range(3):
-            for side in range(2):
-                at = (2 * block + side) * 128
-                ref[at : at + 128, :] = acc[block, rows, side * 128 : side * 128 + 128]
+
+    def block(i, j):
+        rows, columns = i % 2 * 128, j % 2 * 128
+        return acc[i // 2 + j // 2, rows : rows + 128, columns : columns + 128]
+
+    def put(ref, half):
+        for n, (i, j) in enumerate(BLOCKS[half]):
+            value = block(i, j)
+            if i != j and i // 2 == j // 2:
+                value = value + block(j, i).T
+            ref[n * 128 : n * 128 + 128, :] = value
+
+    for core in range(2):
+
+        @pl.when(core_ref[0] == core)
+        def _():
+            put(keep_ref, core)
+            put(send_ref, 1 - core)
 
 
 def gram_halves(core, spectra):
@@ -87,13 +100,16 @@
     return jnp.broadcast_to(group[i : i + 1, :], (8, 128))
 
 
-def eliminate(a, out_ref):
+def eliminate(a, one, out_ref):
     sub = lax.broadcasted_iota(jnp.int32, (8, 128), 0)
-    square = [lanes_of(a[0], 64 + j) for j in range(8)]
+    square = [one * lanes_of(a[0], 64 + j) for j in range(8)]
     for b in range(8):
         lane = 64 + 8 * b
-        nearest = [lanes_of(a[b + 1], lane + j) for j in range(8)] if b < 7 else []
-        following = [lanes_of(a[b + 1], lane + 8 + j) for j in range(8)] if b < 7 else []
+        near = {i: [lanes_of(a[i], lane + j) for j in range(8)] for i in range(b + 1, min(b + 3, 8))}
+        following = []
+        if b < 7:
+            near[b + 1][0] = one * near[b + 1][0]
+            following = [lanes_of(a[b + 1], lane + 8 + j) for j in range(8)]
         rows = a[b]
         scaled = []
         inverse = jnp.zeros((8, 128), F32)
@@ -109,16 +125,19 @@
             inverse = jnp.where(sub == k, inv, inverse)
             if b < 7:
                 scaled.append(row * inv)
-                down = nearest[k] * inv
-                for c in range(k + 1, 8):
-                    nearest[c] = nearest[c] - down * s[c]
-                for c in range(8):
-                    following[c] = following[c] - down * row_of(nearest[k], c)
+                for i, panel in near.items():
+                    down = panel[k] * inv
+                    for c in range(k + 1, 8):
+                        panel[c] = panel[c] - down * s[c]
+                    if i == b + 1:
+                        for c in range(8):
+                            following[c] = following[c] - down * row_of(panel[k], c)
         out_ref[8 * b : 8 * b + 8, :] = rows * (inverse * lax.rsqrt(inverse))
         if b == 7:
             break
-        a[b + 1] = a[b + 1] - tree([nearest[k] * scaled[k] for k in range(8)])
-        panels = {i: [lanes_of(a[i], lane + j) for j in range(8)] for i in range(b + 2, 8)}
+        for i, panel in near.items():
+            a[i] = a[i] - tree([panel[k] * scaled[k] for k in range(8)])
+        panels = {i: [lanes_of(a[i], lane + j) for j in range(8)] for i in range(b + 3, 8)}
         if panels:
             q = rows * inverse
             for k in range(7, 0, -1):
@@ -135,29 +154,26 @@
     core = core_ref[0]
     zero_is_mine = core == 0
 
-    def half(h, block):
-        at = slice(block * 128, block * 128 + 128)
-        a, b = mine_ref[at, :], other_ref[at, :]
-        return jnp.where(zero_is_mine, a, b) if h == 0 else jnp.where(zero_is_mine, b, a)
-
-    def whole(block):
-        return jnp.concatenate(
-            [jnp.concatenate([half(h, 2 * block), half(h, 2 * block + 1)], axis=1) for h in range(2)], axis=0
-        )
-
     def put(i, j, value):
-        at = (slice(256 * i, 256 * i + 256), slice(256 * j, 256 * j + 256))
-        gh[at], gl[at] = split(value * 2.0**-20)
-
-    t0, t1, t2 = whole(0), whole(1), whole(2)
-    put(0, 0, t0 + t0.T)
-    put(0, 1, t1)
-    put(1, 0, t1.T)
-    put(1, 1, t2 + t2.T)
-
+        at = (slice(128 * i, 128 * i + 128), slice(128 * j, 128 * j + 128))
+        gh[at], gl[at] = split(value)
+
+    for half in range(2):
+        first, second = (mine_ref, other_ref) if half == 0 else (other_ref, mine_ref)
+        for n, (i, j) in enumerate(BLOCKS[half]):
+            at = slice(n * 128, n * 128 + 128)
+            value = jnp.where(zero_is_mine, first[at, :], second[at, :]) * 2.0**-20
+            flipped = value.T
+            if i == j:
+                value = value + flipped
+            else:
+                put(j, i, flipped)
+            put(i, j, value)
     basis[...] = start_ref[...]
     lanes = lax.broadcasted_iota(jnp.int32, (K, 128), 1)
     eye = (lanes == lax.broadcasted_iota(jnp.int32, (K, 128), 0)).astype(F32)
+
+    one = jnp.where(core >= 0, 1.0, 0.0)
 
     def step(_, carry):
         bh, bl = split(basis[...])
@@ -167,7 +183,7 @@
         first = mul(jnp.concatenate([ih, il], axis=0), jnp.concatenate([il, ih], axis=0), NT)
         cross = first[:K] + first[K:] + mul(ih, jnp.concatenate([ih, il], axis=0), NT)
         a = jnp.where(lanes < K, eye, cross)
-        eliminate([a[8 * i : 8 * i + 8, :] for i in range(8)], rp)
+        eliminate([a[8 * i : 8 * i + 8, :] for i in range(8)], one, rp)
         xh, xl = split(rp[:, :K])
         both = mul(jnp.concatenate([xh, xl], axis=0), ih, NN)
         basis[...] = both[:K] + both[K:] + mul(xh, il, NN)
@@ -225,7 +241,7 @@
     core = lax.axis_index("core").astype(jnp.int32).reshape(1)
     keep, send = gram_halves(core, spectra)
     part = keep + swap(send)
-    part = lax.all_to_all(part.reshape(raster, HALF // raster, 128), "raster", 0, 0)
+    part = lax.all_to_all(part.reshape(raster, 1, HALF * 128 // raster), "raster", 0, 0)
     piece = jnp.sum(part, axis=0)
     piece = jnp.sum(spread(piece, "z", z), axis=0)
     mine = spread(piece, "raster", raster).reshape(HALF, 128)

time: 89 us -> 84.8 us (0.953)
  blocking collectives: 51 us -> 49.2 us
  Pallas kernels: 18.9 us -> 17.3 us
    pallas_call x1, Pallas kernels: 14.9 us -> 13.2 us  [finish(): pl.pallas_call(iterate_kernel, in_specs=[pl.BlockSpec(memory_space=pltpu....]
    all_to_all x1, blocking collectives: 15.9 us -> 14.6 us  [body(): lax.all_to_all(part.reshape(raster, 1, HALF * 128 // raster), 'raster', 0...]
where the time goes in v3:
time: 84.8 us; the launch traced here: 84.5 us
  blocking collectives  49.2 us (58%)
  Pallas kernels  17.3 us (20%)
  starting transfers between devices  15.1 us (18%)
  waiting for transfers between devices  2.47 us (3%)
    all_to_all x2, blocking collectives, spread(): lax.all_to_all(jnp.broadcast_to(piece[None], (copies, *piece.shape)), axi...  34.6 us
    ppermute x2, starting transfers between devices, swap(): return lax.ppermute(value, 'core', [(0, 1), (1, 0)])  15.1 us
    all_to_all x1, blocking collectives, body(): lax.all_to_all(part.reshape(raster, 1, HALF * 128 // raster), 'raster', 0...  14.6 us
    pallas_call x1, Pallas kernels, finish(): pl.pallas_call(iterate_kernel, in_specs=[pl.BlockSpec(memory_space=pltpu....  13.2 us
    pallas_call x1, Pallas kernels, gram_halves(): pl.pallas_call(gram_kernel, in_specs=[pl.BlockSpec(memory_space=pltpu.SME...  4.07 us
    ppermute x2, waiting for transfers between devices, swap(): return lax.ppermute(value, 'core', [(0, 1), (1, 0)])  2.47 us
  transfers between devices with their start and end apart: 2, of which 2 were waited for; matrix products, arithmetic and copies ran while one was open for 0% of the time, Pallas kernels for 0%

profile of v3, /device:TPU:1, one launch (start us, length us, event | category | flops | bytes accessed | tf_op | source)
XLA Modules:
  0.0 84.5 jit_solution(10298272982740121890)
XLA Ops:
  0.0 0.0 copy-start
  0.0 4.1 %shard_map.28 = (f32[640,128]{1,0:T(8,128)S(1)}, f32[640,128]{1,0:T(8,128)S(1)}) custom-call(s32[1]{0:T(128)} %bitcast.core_ref, f32[2048,512]{1,0:T(8,128)} %spectra_ref.3), custom_call_target="tpu_custom_call" | custom-call | tf_op jit(solution)/shard_map/pallas_call | solution.py:75
  4.1 8.8 %collective-permute-start = (f32[640,128]{1,0:T(8,128)S(1)}, f32[640,128]{1,0:T(8,128)S(1)}, u32[]{:S(2)}, u32[]{:S(2)}) collective-permute-start(f32[640,128]{1,0:T(8,128)S(1)} %get-tuple-element.8), channel_id=1, source_target_pairs={{0,1},{1,0},{2,3},{3,2},{4,5},{5,4},{6,7},{7,6},{8,9},{9,8},{10,11... | collective-permute-start | bytes 983048 | tf_op jit(solution)/shard_map/ppermute | solution.py:233
  12.9 1.2 %collective-permute-done = f32[640,128]{1,0:T(8,128)S(1)} collective-permute-done((f32[640,128]{1,0:T(8,128)S(1)}, f32[640,128]{1,0:T(8,128)S(1)}, u32[]{:S(2)}, u32[]{:S(2)}) %collective-permute-start) | collective-permute-done | bytes 327712 | tf_op jit(solution)/shard_map/ppermute | solution.py:233
  14.1 14.6 %all_to_all.15 = f32[32,1,2560]{2,1,0:T(1,128)S(1)} all-to-all(f32[32,1,2560]{2,1,0:T(1,128)S(1)} %bitcast.8), channel_id=1, replica_groups=mesh['raster'=32,'z'=8,'core'=2] {'raster'}, dimensions={0} | all-to-all | bytes 655360 | tf_op jit(solution)/shard_map/all_to_all | solution.py:244
  28.7 0.2 reduce_sum.18
  28.9 17.2 %all_to_all.16 = f32[8,1,2560]{2,1,0:T(1,128)S(1)} all-to-all(f32[8,1,2560]{2,1,0:T(1,128)S(1)} %broadcast_in_dim.4), channel_id=1, replica_groups=mesh['raster'=32,'z'=8,'core'=2] {'z'}, dimensions={0} | all-to-all | bytes 163840 | tf_op jit(solution)/shard_map/all_to_all | solution.py:237
  46.2 0.1 reduce_sum.19
  46.2 0.2 broadcast_in_dim.5
  46.4 17.4 %all_to_all.17 = f32[32,1,2560]{2,1,0:T(1,128)S(1)} all-to-all(f32[32,1,2560]{2,1,0:T(1,128)S(1)} %broadcast_in_dim.5), channel_id=1, replica_groups=mesh['raster'=32,'z'=8,'core'=2] {'raster'}, dimensions={0} | all-to-all | bytes 655360 | tf_op jit(solution)/shard_map/all_to_all | solution.py:237
  63.8 6.3 %collective-permute-start.1 = (f32[640,128]{1,0:T(8,128)S(1)}, f32[640,128]{1,0:T(8,128)S(1)}, u32[]{:S(2)}, u32[]{:S(2)}) collective-permute-start(f32[640,128]{1,0:T(8,128)S(1)} %bitcast.5), channel_id=1, source_target_pairs={{0,1},{1,0},{2,3},{3,2},{4,5},{5,4},{6,7},{7,6},{8,9},{9,8},{10,11... | collective-permute-start | bytes 983048 | tf_op jit(solution)/shard_map/ppermute | solution.py:233
  70.1 1.2 %collective-permute-done.1.other_ref = f32[640,128]{1,0:T(8,128)S(1)} collective-permute-done((f32[640,128]{1,0:T(8,128)S(1)}, f32[640,128]{1,0:T(8,128)S(1)}, u32[]{:S(2)}, u32[]{:S(2)}) %collective-permute-start.1) | collective-permute-done | bytes 327712 | tf_op jit(solution)/shard_map/ppermute | solution.py:233
  71.3 0.0 copy-done
  71.4 13.2 %shard_map.29 = f32[64,2048]{1,0:T(8,128)} custom-call(s32[1]{0:T(128)} %bitcast.core_ref, f32[640,128]{1,0:T(8,128)S(1)} %bitcast.6, f32[640,128]{1,0:T(8,128)S(1)} %collective-permute-done.1.other_ref, f32[64,512]{1,0:T(8,128)S(1)} %bitcast.7, f32[2048,512]{1,0:T(8,128)} %spectra_ref.3), custom_call_target="tpu_custom_call" | custom-call | tf_op jit(solution)/shard_map/pallas_call | solution.py:213
  (2 shorter events, 0.1 us)
Async XLA Ops:
  0.0 71.4 %copy-start = (f32[512,64]{0,1:T(8,128)S(1)}, f32[512,64]{0,1:T(8,128)}, u32[]{:S(2)}) copy-start(f32[512,64]{0,1:T(8,128)} %param.3) | copy-start | bytes 393220
  4.1 10.0 %collective-permute-start = (f32[640,128]{1,0:T(8,128)S(1)}, f32[640,128]{1,0:T(8,128)S(1)}, u32[]{:S(2)}, u32[]{:S(2)}) collective-permute-start(f32[640,128]{1,0:T(8,128)S(1)} %get-tuple-element.8), channel_id=1, source_target_pairs={{0,1},{1,0},{2,3},{3,2},{4,5},{5,4},{6,7},{7,6},{8,9},{9,8},{10,11... | collective-permute-start | bytes 983048 | tf_op jit(solution)/shard_map/ppermute | solution.py:233
  63.8 7.6 %collective-permute-start.1 = (f32[640,128]{1,0:T(8,128)S(1)}, f32[640,128]{1,0:T(8,128)S(1)}, u32[]{:S(2)}, u32[]{:S(2)}) collective-permute-start(f32[640,128]{1,0:T(8,128)S(1)} %bitcast.5), channel_id=1, source_target_pairs={{0,1},{1,0},{2,3},{3,2},{4,5},{5,4},{6,7},{7,6},{8,9},{9,8},{10,11... | collective-permute-start | bytes 983048 | tf_op jit(solution)/shard_map/ppermute | solution.py:233

commit v4 on v3

--- a/solution.py
+++ b/solution.py
@@ -105,46 +105,42 @@
     square = [one * lanes_of(a[0], 64 + j) for j in range(8)]
     for b in range(8):
         lane = 64 + 8 * b
-        near = {i: [lanes_of(a[i], lane + j) for j in range(8)] for i in range(b + 1, min(b + 3, 8))}
+        panels = {i: [lanes_of(a[i], lane + j) for j in range(8)] for i in range(b + 1, 8)}
         following = []
         if b < 7:
-            near[b + 1][0] = one * near[b + 1][0]
+            panels[b + 1][0] = one * panels[b + 1][0]
             following = [lanes_of(a[b + 1], lane + 8 + j) for j in range(8)]
         rows = a[b]
-        scaled = []
         inverse = jnp.zeros((8, 128), F32)
-        for k in range(8):
-            s = {c: row_of(square[k], c) for c in range(k, 8)}
-            inv = pl.reciprocal(s[k], approx=True)
-            below = jnp.where(sub > k, square[k], 0.0)
-            down = below * inv
-            for c in range(k + 1, 8):
-                square[c] = square[c] - ((below * s[c]) * inv if c == k + 1 else down * s[c])
-            row = row_of(rows, k)
-            rows = rows - down * row
-            inverse = jnp.where(sub == k, inv, inverse)
-            if b < 7:
-                scaled.append(row * inv)
-                for i, panel in near.items():
+        for p in range(0, 8, 2):
+            q = p + 1
+            first = {c: row_of(square[p], c) for c in range(p, 8)}
+            second = {c: row_of(square[q], c) for c in range(q, 8)}
+            cofactor = pl.reciprocal(first[p] * second[q] - first[q] * first[q], approx=True)
+            invs = (pl.reciprocal(first[p], approx=True), first[p] * cofactor)
+            for c in range(q + 1, min(q + 3, 8)):
+                left = second[q] * first[c] - first[q] * second[c]
+                right = first[p] * second[c] - first[q] * first[c]
+                square[c] = square[c] - (square[p] * left + square[q] * right) * cofactor
+            downs = [jnp.where(sub > p, square[p], 0.0) * invs[0]]
+            square[q] = square[q] - downs[0] * first[q]
+            downs.append(jnp.where(sub > q, square[q], 0.0) * invs[1])
+            second = {c: row_of(square[q], c) for c in range(q + 1, 8)}
+            for c in range(q + 3, 8):
+                square[c] = (square[c] - downs[0] * first[c]) - downs[1] * second[c]
+            for k, s, inv, down in zip((p, q), (first, second), invs, downs):
+                row = row_of(rows, k)
+                rows = rows - down * row
+                inverse = jnp.where(sub == k, inv, inverse)
+                for i, panel in panels.items():
                     down = panel[k] * inv
                     for c in range(k + 1, 8):
                         panel[c] = panel[c] - down * s[c]
                     if i == b + 1:
                         for c in range(8):
                             following[c] = following[c] - down * row_of(panel[k], c)
+                    a[i] = a[i] - down * row
         out_ref[8 * b : 8 * b + 8, :] = rows * (inverse * lax.rsqrt(inverse))
-        if b == 7:
-            break
-        for i, panel in near.items():
-            a[i] = a[i] - tree([panel[k] * scaled[k] for k in range(8)])
-        panels = {i: [lanes_of(a[i], lane + j) for j in range(8)] for i in range(b + 3, 8)}
-        if panels:
-            q = rows * inverse
-            for k in range(7, 0, -1):
-                q = q - jnp.where(sub < k, square[k] * inverse, 0.0) * row_of(q, k)
-            q = [row_of(q, c) for c in range(8)]
-            for i, panel in panels.items():
-                a[i] = a[i] - tree([panel[c] * q[c] for c in range(8)])
         square = following
 
 
@@ -169,24 +165,27 @@
             else:
                 put(j, i, flipped)
             put(i, j, value)
-    basis[...] = start_ref[...]
+    def times_gram(high, low):
+        both = mul(jnp.concatenate([high, low], axis=0), gh[...], NN)
+        return both[:K] + both[K:] + mul(high, gl[...], NN)
+
+    basis[...] = times_gram(*split(start_ref[...]))
     lanes = lax.broadcasted_iota(jnp.int32, (K, 128), 1)
     eye = (lanes == lax.broadcasted_iota(jnp.int32, (K, 128), 0)).astype(F32)
 
     one = jnp.where(core >= 0, 1.0, 0.0)
 
-    def step(_, carry):
-        bh, bl = split(basis[...])
-        both = mul(jnp.concatenate([bh, bl], axis=0), gh[...], NN)
-        image = both[:K] + both[K:] + mul(bh, gl[...], NN)
+    def step(count, carry):
+        image = basis[...]
         ih, il = split(image)
         first = mul(jnp.concatenate([ih, il], axis=0), jnp.concatenate([il, ih], axis=0), NT)
         cross = first[:K] + first[K:] + mul(ih, jnp.concatenate([ih, il], axis=0), NT)
         a = jnp.where(lanes < K, eye, cross)
+        wh, wl = split(jnp.where(count == ITERS - 1, image, times_gram(ih, il)))
         eliminate([a[8 * i : 8 * i + 8, :] for i in range(8)], one, rp)
         xh, xl = split(rp[:, :K])
-        both = mul(jnp.concatenate([xh, xl], axis=0), ih, NN)
-        basis[...] = both[:K] + both[K:] + mul(xh, il, NN)
+        both = mul(jnp.concatenate([xh, xl], axis=0), wh, NN)
+        basis[...] = both[:K] + both[K:] + mul(xh, wl, NN)
         return carry
 
     lax.fori_loop(0, ITERS, step, 0)

time: 84.8 us -> 82.7 us (0.975)
  Pallas kernels: 17.3 us -> 15.2 us
    pallas_call x1, Pallas kernels: 13.2 us -> 11.1 us  [finish(): pl.pallas_call(iterate_kernel, in_specs=[pl.BlockSpec(memory_space=pltpu....]
where the time goes in v4:
time: 82.7 us; the launch traced here: 82.4 us
  blocking collectives  49.2 us (59%)
  Pallas kernels  15.2 us (18%)
  starting transfers between devices  15.1 us (18%)
  waiting for transfers between devices  2.47 us (3%)
    all_to_all x2, blocking collectives, spread(): lax.all_to_all(jnp.broadcast_to(piece[None], (copies, *piece.shape)), axi...  34.6 us
    ppermute x2, starting transfers between devices, swap(): return lax.ppermute(value, 'core', [(0, 1), (1, 0)])  15.1 us
    all_to_all x1, blocking collectives, body(): lax.all_to_all(part.reshape(raster, 1, HALF * 128 // raster), 'raster', 0...  14.6 us
    pallas_call x1, Pallas kernels, finish(): pl.pallas_call(iterate_kernel, in_specs=[pl.BlockSpec(memory_space=pltpu....  11.1 us
    pallas_call x1, Pallas kernels, gram_halves(): pl.pallas_call(gram_kernel, in_specs=[pl.BlockSpec(memory_space=pltpu.SME...  4.07 us
    ppermute x2, waiting for transfers between devices, swap(): return lax.ppermute(value, 'core', [(0, 1), (1, 0)])  2.47 us
  transfers between devices with their start and end apart: 2, of which 2 were waited for; matrix products, arithmetic and copies ran while one was open for 0% of the time, Pallas kernels for 0%

profile of v4, /device:TPU:1, one launch (start us, length us, event | category | flops | bytes accessed | tf_op | source)
XLA Modules:
  0.0 82.4 jit_solution(10493736118006729544)
XLA Ops:
  0.0 0.0 copy-start
  0.0 4.1 %shard_map.28 = (f32[640,128]{1,0:T(8,128)S(1)}, f32[640,128]{1,0:T(8,128)S(1)}) custom-call(s32[1]{0:T(128)} %bitcast.core_ref, f32[2048,512]{1,0:T(8,128)} %spectra_ref.3), custom_call_target="tpu_custom_call" | custom-call | tf_op jit(solution)/shard_map/pallas_call | solution.py:75
  4.1 8.8 %collective-permute-start = (f32[640,128]{1,0:T(8,128)S(1)}, f32[640,128]{1,0:T(8,128)S(1)}, u32[]{:S(2)}, u32[]{:S(2)}) collective-permute-start(f32[640,128]{1,0:T(8,128)S(1)} %get-tuple-element.8), channel_id=1, source_target_pairs={{0,1},{1,0},{2,3},{3,2},{4,5},{5,4},{6,7},{7,6},{8,9},{9,8},{10,11... | collective-permute-start | bytes 983048 | tf_op jit(solution)/shard_map/ppermute | solution.py:232
  12.9 1.2 %collective-permute-done = f32[640,128]{1,0:T(8,128)S(1)} collective-permute-done((f32[640,128]{1,0:T(8,128)S(1)}, f32[640,128]{1,0:T(8,128)S(1)}, u32[]{:S(2)}, u32[]{:S(2)}) %collective-permute-start) | collective-permute-done | bytes 327712 | tf_op jit(solution)/shard_map/ppermute | solution.py:232
  14.1 14.6 %all_to_all.15 = f32[32,1,2560]{2,1,0:T(1,128)S(1)} all-to-all(f32[32,1,2560]{2,1,0:T(1,128)S(1)} %bitcast.8), channel_id=1, replica_groups=mesh['raster'=32,'z'=8,'core'=2] {'raster'}, dimensions={0} | all-to-all | bytes 655360 | tf_op jit(solution)/shard_map/all_to_all | solution.py:243
  28.7 0.2 reduce_sum.18
  28.9 17.2 %all_to_all.16 = f32[8,1,2560]{2,1,0:T(1,128)S(1)} all-to-all(f32[8,1,2560]{2,1,0:T(1,128)S(1)} %broadcast_in_dim.4), channel_id=1, replica_groups=mesh['raster'=32,'z'=8,'core'=2] {'z'}, dimensions={0} | all-to-all | bytes 163840 | tf_op jit(solution)/shard_map/all_to_all | solution.py:236
  46.2 0.1 reduce_sum.19
  46.2 0.2 broadcast_in_dim.5
  46.4 17.4 %all_to_all.17 = f32[32,1,2560]{2,1,0:T(1,128)S(1)} all-to-all(f32[32,1,2560]{2,1,0:T(1,128)S(1)} %broadcast_in_dim.5), channel_id=1, replica_groups=mesh['raster'=32,'z'=8,'core'=2] {'raster'}, dimensions={0} | all-to-all | bytes 655360 | tf_op jit(solution)/shard_map/all_to_all | solution.py:236
  63.8 6.3 %collective-permute-start.1 = (f32[640,128]{1,0:T(8,128)S(1)}, f32[640,128]{1,0:T(8,128)S(1)}, u32[]{:S(2)}, u32[]{:S(2)}) collective-permute-start(f32[640,128]{1,0:T(8,128)S(1)} %bitcast.5), channel_id=1, source_target_pairs={{0,1},{1,0},{2,3},{3,2},{4,5},{5,4},{6,7},{7,6},{8,9},{9,8},{10,11... | collective-permute-start | bytes 983048 | tf_op jit(solution)/shard_map/ppermute | solution.py:232
  70.1 1.2 %collective-permute-done.1.other_ref = f32[640,128]{1,0:T(8,128)S(1)} collective-permute-done((f32[640,128]{1,0:T(8,128)S(1)}, f32[640,128]{1,0:T(8,128)S(1)}, u32[]{:S(2)}, u32[]{:S(2)}) %collective-permute-start.1) | collective-permute-done | bytes 327712 | tf_op jit(solution)/shard_map/ppermute | solution.py:232
  71.3 0.0 copy-done
  71.4 11.1 %shard_map.29 = f32[64,2048]{1,0:T(8,128)} custom-call(s32[1]{0:T(128)} %bitcast.core_ref, f32[640,128]{1,0:T(8,128)S(1)} %bitcast.6, f32[640,128]{1,0:T(8,128)S(1)} %collective-permute-done.1.other_ref, f32[64,512]{1,0:T(8,128)S(1)} %bitcast.7, f32[2048,512]{1,0:T(8,128)} %spectra_ref.3), custom_call_target="tpu_custom_call" | custom-call | tf_op jit(solution)/shard_map/pallas_call | solution.py:212
  (2 shorter events, 0.1 us)
Async XLA Ops:
  0.0 71.4 %copy-start = (f32[512,64]{0,1:T(8,128)S(1)}, f32[512,64]{0,1:T(8,128)}, u32[]{:S(2)}) copy-start(f32[512,64]{0,1:T(8,128)} %param.3) | copy-start | bytes 393220
  4.1 10.0 %collective-permute-start = (f32[640,128]{1,0:T(8,128)S(1)}, f32[640,128]{1,0:T(8,128)S(1)}, u32[]{:S(2)}, u32[]{:S(2)}) collective-permute-start(f32[640,128]{1,0:T(8,128)S(1)} %get-tuple-element.8), channel_id=1, source_target_pairs={{0,1},{1,0},{2,3},{3,2},{4,5},{5,4},{6,7},{7,6},{8,9},{9,8},{10,11... | collective-permute-start | bytes 983048 | tf_op jit(solution)/shard_map/ppermute | solution.py:232
  63.8 7.6 %collective-permute-start.1 = (f32[640,128]{1,0:T(8,128)S(1)}, f32[640,128]{1,0:T(8,128)S(1)}, u32[]{:S(2)}, u32[]{:S(2)}) collective-permute-start(f32[640,128]{1,0:T(8,128)S(1)} %bitcast.5), channel_id=1, source_target_pairs={{0,1},{1,0},{2,3},{3,2},{4,5},{5,4},{6,7},{7,6},{8,9},{9,8},{10,11... | collective-permute-start | bytes 983048 | tf_op jit(solution)/shard_map/ppermute | solution.py:232

commit v5 on v4

--- a/solution.py
+++ b/solution.py
@@ -11,8 +11,8 @@
 K = 64
 ITERS = 6
 CHUNK = 512
-HALF = 5 * 128
-BLOCKS = (((0, 0), (0, 1), (0, 2), (0, 3), (3, 3)), ((1, 1), (1, 2), (1, 3), (2, 2), (2, 3)))
+HALF = 3 * 128 + 3 * 64
+OFF = (((0, 1), (0, 2), (0, 3)), ((1, 2), (1, 3), (2, 3)))
 F32 = jnp.float32
 BF16 = jnp.bfloat16
 NN = (((1,), (0,)), ((), ()))
@@ -54,11 +54,19 @@
         return acc[i // 2 + j // 2, rows : rows + 128, columns : columns + 128]
 
     def put(ref, half):
-        for n, (i, j) in enumerate(BLOCKS[half]):
+        for n, (i, j) in enumerate(OFF[half]):
             value = block(i, j)
-            if i != j and i // 2 == j // 2:
+            if i // 2 == j // 2:
                 value = value + block(j, i).T
             ref[n * 128 : n * 128 + 128, :] = value
+        right = lax.broadcasted_iota(jnp.int32, (64, 128), 1) >= 64
+        corners = []
+        for n, i in enumerate((2 * half, 2 * half + 1)):
+            value = block(i, i)
+            at = 384 + n * 64
+            ref[at : at + 64, :] = value[:64] + jnp.where(right, value.T[:64], 0.0)
+            corners.append(value[64:])
+        ref[512:576, :] = jnp.where(right, corners[1], pltpu.roll(corners[0], 64, 1))
 
     for core in range(2):
 
@@ -154,17 +162,24 @@
         at = (slice(128 * i, 128 * i + 128), slice(128 * j, 128 * j + 128))
         gh[at], gl[at] = split(value)
 
+    right = lax.broadcasted_iota(jnp.int32, (64, 128), 1) >= 64
     for half in range(2):
         first, second = (mine_ref, other_ref) if half == 0 else (other_ref, mine_ref)
-        for n, (i, j) in enumerate(BLOCKS[half]):
-            at = slice(n * 128, n * 128 + 128)
-            value = jnp.where(zero_is_mine, first[at, :], second[at, :]) * 2.0**-20
-            flipped = value.T
-            if i == j:
-                value = value + flipped
-            else:
-                put(j, i, flipped)
+
+        def rows_at(start, count):
+            at = slice(start, start + count)
+            return jnp.where(zero_is_mine, first[at, :], second[at, :]) * 2.0**-20
+
+        for n, (i, j) in enumerate(OFF[half]):
+            value = rows_at(n * 128, 128)
             put(i, j, value)
+            put(j, i, value.T)
+        corners = rows_at(512, 64)
+        for n, i in enumerate((2 * half, 2 * half + 1)):
+            corner = jnp.where(right, corners if n else pltpu.roll(corners, 64, 1), 0.0)
+            value = jnp.concatenate([rows_at(384 + n * 64, 64), corner], axis=0)
+            put(i, i, value + value.T)
+
     def times_gram(high, low):
         both = mul(jnp.concatenate([high, low], axis=0), gh[...], NN)
         return both[:K] + both[K:] + mul(high, gl[...], NN)

time: 82.7 us -> 82.4 us (level)
  blocking collectives: 49.2 us -> 48.1 us
    ppermute x2, starting transfers between devices: 15.1 us -> 15.9 us  [swap(): return lax.ppermute(value, 'core', [(0, 1), (1, 0)])]
where the time goes in v5:
time: 82.4 us; the launch traced here: 82.2 us
  blocking collectives  48.1 us (58%)
  starting transfers between devices  15.9 us (19%)
  Pallas kernels  15.3 us (19%)
  waiting for transfers between devices  2.37 us (3%)
    all_to_all x2, blocking collectives, spread(): lax.all_to_all(jnp.broadcast_to(piece[None], (copies, *piece.shape)), axi...  33.8 us
    ppermute x2, starting transfers between devices, swap(): return lax.ppermute(value, 'core', [(0, 1), (1, 0)])  15.9 us
    all_to_all x1, blocking collectives, body(): lax.all_to_all(part.reshape(raster, 1, HALF * 128 // raster), 'raster', 0...  14.3 us
    pallas_call x1, Pallas kernels, finish(): pl.pallas_call(iterate_kernel, in_specs=[pl.BlockSpec(memory_space=pltpu....  11.1 us
    pallas_call x1, Pallas kernels, gram_halves(): pl.pallas_call(gram_kernel, in_specs=[pl.BlockSpec(memory_space=pltpu.SME...  4.19 us
    ppermute x2, waiting for transfers between devices, swap(): return lax.ppermute(value, 'core', [(0, 1), (1, 0)])  2.37 us
  transfers between devices with their start and end apart: 2, of which 2 were waited for; matrix products, arithmetic and copies ran while one was open for 0% of the time, Pallas kernels for 0%

profile of v5, /device:TPU:1, one launch (start us, length us, event | category | flops | bytes accessed | tf_op | source)
XLA Modules:
  0.0 82.2 jit_solution(9339647627002153094)
XLA Ops:
  0.0 0.0 copy-start
  0.0 4.2 %shard_map.28 = (f32[576,128]{1,0:T(8,128)S(1)}, f32[576,128]{1,0:T(8,128)S(1)}) custom-call(s32[1]{0:T(128)} %bitcast.core_ref, f32[2048,512]{1,0:T(8,128)} %spectra_ref.3), custom_call_target="tpu_custom_call" | custom-call | tf_op jit(solution)/shard_map/pallas_call | solution.py:83
  4.2 8.8 %collective-permute-start = (f32[576,128]{1,0:T(8,128)S(1)}, f32[576,128]{1,0:T(8,128)S(1)}, u32[]{:S(2)}, u32[]{:S(2)}) collective-permute-start(f32[576,128]{1,0:T(8,128)S(1)} %get-tuple-element.8), channel_id=1, source_target_pairs={{0,1},{1,0},{2,3},{3,2},{4,5},{5,4},{6,7},{7,6},{8,9},{9,8},{10,11... | collective-permute-start | bytes 884744 | tf_op jit(solution)/shard_map/ppermute | solution.py:247
  13.0 1.2 %collective-permute-done = f32[576,128]{1,0:T(8,128)S(1)} collective-permute-done((f32[576,128]{1,0:T(8,128)S(1)}, f32[576,128]{1,0:T(8,128)S(1)}, u32[]{:S(2)}, u32[]{:S(2)}) %collective-permute-start) | collective-permute-done | bytes 294944 | tf_op jit(solution)/shard_map/ppermute | solution.py:247
  14.2 14.3 %all_to_all.15 = f32[32,1,2304]{2,1,0:T(1,128)S(1)} all-to-all(f32[32,1,2304]{2,1,0:T(1,128)S(1)} %bitcast.8), channel_id=1, replica_groups=mesh['raster'=32,'z'=8,'core'=2] {'raster'}, dimensions={0} | all-to-all | bytes 589824 | tf_op jit(solution)/shard_map/all_to_all | solution.py:258
  28.5 0.2 reduce_sum.18
  28.7 17.2 %all_to_all.16 = f32[8,1,2304]{2,1,0:T(1,128)S(1)} all-to-all(f32[8,1,2304]{2,1,0:T(1,128)S(1)} %broadcast_in_dim.4), channel_id=1, replica_groups=mesh['raster'=32,'z'=8,'core'=2] {'z'}, dimensions={0} | all-to-all | bytes 147456 | tf_op jit(solution)/shard_map/all_to_all | solution.py:251
  45.8 0.1 reduce_sum.19
  45.9 0.2 broadcast_in_dim.5
  46.1 16.7 %all_to_all.17 = f32[32,1,2304]{2,1,0:T(1,128)S(1)} all-to-all(f32[32,1,2304]{2,1,0:T(1,128)S(1)} %broadcast_in_dim.5), channel_id=1, replica_groups=mesh['raster'=32,'z'=8,'core'=2] {'raster'}, dimensions={0} | all-to-all | bytes 589824 | tf_op jit(solution)/shard_map/all_to_all | solution.py:251
  62.7 7.2 %collective-permute-start.1 = (f32[576,128]{1,0:T(8,128)S(1)}, f32[576,128]{1,0:T(8,128)S(1)}, u32[]{:S(2)}, u32[]{:S(2)}) collective-permute-start(f32[576,128]{1,0:T(8,128)S(1)} %bitcast.5), channel_id=1, source_target_pairs={{0,1},{1,0},{2,3},{3,2},{4,5},{5,4},{6,7},{7,6},{8,9},{9,8},{10,11... | collective-permute-start | bytes 884744 | tf_op jit(solution)/shard_map/ppermute | solution.py:247
  69.9 1.2 %collective-permute-done.1.other_ref = f32[576,128]{1,0:T(8,128)S(1)} collective-permute-done((f32[576,128]{1,0:T(8,128)S(1)}, f32[576,128]{1,0:T(8,128)S(1)}, u32[]{:S(2)}, u32[]{:S(2)}) %collective-permute-start.1) | collective-permute-done | bytes 294944 | tf_op jit(solution)/shard_map/ppermute | solution.py:247
  71.1 0.0 copy-done
  71.1 11.1 %shard_map.29 = f32[64,2048]{1,0:T(8,128)} custom-call(s32[1]{0:T(128)} %bitcast.core_ref, f32[576,128]{1,0:T(8,128)S(1)} %bitcast.6, f32[576,128]{1,0:T(8,128)S(1)} %collective-permute-done.1.other_ref, f32[64,512]{1,0:T(8,128)S(1)} %bitcast.7, f32[2048,512]{1,0:T(8,128)} %spectra_ref.3), custom_call_target="tpu_custom_call" | custom-call | tf_op jit(solution)/shard_map/pallas_call | solution.py:227
  (2 shorter events, 0.1 us)
Async XLA Ops:
  0.0 71.1 %copy-start = (f32[512,64]{0,1:T(8,128)S(1)}, f32[512,64]{0,1:T(8,128)}, u32[]{:S(2)}) copy-start(f32[512,64]{0,1:T(8,128)} %param.3) | copy-start | bytes 393220
  4.2 10.0 %collective-permute-start = (f32[576,128]{1,0:T(8,128)S(1)}, f32[576,128]{1,0:T(8,128)S(1)}, u32[]{:S(2)}, u32[]{:S(2)}) collective-permute-start(f32[576,128]{1,0:T(8,128)S(1)} %get-tuple-element.8), channel_id=1, source_target_pairs={{0,1},{1,0},{2,3},{3,2},{4,5},{5,4},{6,7},{7,6},{8,9},{9,8},{10,11... | collective-permute-start | bytes 884744 | tf_op jit(solution)/shard_map/ppermute | solution.py:247
  62.7 8.3 %collective-permute-start.1 = (f32[576,128]{1,0:T(8,128)S(1)}, f32[576,128]{1,0:T(8,128)S(1)}, u32[]{:S(2)}, u32[]{:S(2)}) collective-permute-start(f32[576,128]{1,0:T(8,128)S(1)} %bitcast.5), channel_id=1, source_target_pairs={{0,1},{1,0},{2,3},{3,2},{4,5},{5,4},{6,7},{7,6},{8,9},{9,8},{10,11... | collective-permute-start | bytes 884744 | tf_op jit(solution)/shard_map/ppermute | solution.py:247

commit v6 on v5

--- a/solution.py
+++ b/solution.py
@@ -10,7 +10,8 @@
 W = 512
 K = 64
 ITERS = 6
-CHUNK = 512
+NEAR = (5, 8, 8, 8, 8, 8, 8, 8)
+CHUNKS = (256, 768, 1024)
 HALF = 3 * 128 + 3 * 64
 OFF = (((0, 1), (0, 2), (0, 3)), ((1, 2), (1, 3), (2, 3)))
 F32 = jnp.float32
@@ -30,15 +31,16 @@
 
 
 def gram_kernel(core_ref, spectra_ref, keep_ref, send_ref, buf, acc, sems):
-    parts = buf.shape[0] // CHUNK
     loads = []
-    for i in range(parts):
-        at = slice(i * CHUNK, i * CHUNK + CHUNK)
-        loads.append(pltpu.make_async_copy(spectra_ref.at[at], buf.at[at], sems.at[i]))
-        loads[-1].start()
-    for i in range(parts):
-        loads[i].wait()
-        high, low = split(buf[i * CHUNK : i * CHUNK + CHUNK, :])
+    start = 0
+    for n, rows in enumerate(CHUNKS):
+        at = slice(start, start + rows)
+        start += rows
+        loads.append((at, pltpu.make_async_copy(spectra_ref.at[at], buf.at[at], sems.at[n])))
+        loads[-1][1].start()
+    for n, (at, load) in enumerate(loads):
+        load.wait()
+        high, low = split(buf[at, :])
         h0, h1 = high[:, :256], high[:, 256:]
         l0, l1 = low[:, :256], low[:, 256:]
         sums = (
@@ -47,7 +49,7 @@
             0.5 * mul(h1, h1, TN) + mul(h1, l1, TN),
         )
         for block in range(3):
-            acc[block] = acc[block] + sums[block] if i else sums[block]
+            acc[block] = acc[block] + sums[block] if n else sums[block]
 
     def block(i, j):
         rows, columns = i % 2 * 128, j % 2 * 128
@@ -88,7 +90,7 @@
         scratch_shapes=[
             pltpu.VMEM((rows, W), F32),
             pltpu.VMEM((3, 256, 256), F32),
-            pltpu.SemaphoreType.DMA((rows // CHUNK,)),
+            pltpu.SemaphoreType.DMA((len(CHUNKS),)),
         ],
         compiler_params=pltpu.CompilerParams(vmem_limit_bytes=52 * 1024 * 1024),
     )(core, spectra)
@@ -113,13 +115,14 @@
     square = [one * lanes_of(a[0], 64 + j) for j in range(8)]
     for b in range(8):
         lane = 64 + 8 * b
-        panels = {i: [lanes_of(a[i], lane + j) for j in range(8)] for i in range(b + 1, 8)}
+        panels = {i: [lanes_of(a[i], lane + j) for j in range(8)] for i in range(b + 1, min(b + NEAR[b], 8))}
         following = []
         if b < 7:
             panels[b + 1][0] = one * panels[b + 1][0]
             following = [lanes_of(a[b + 1], lane + 8 + j) for j in range(8)]
         rows = a[b]
         inverse = jnp.zeros((8, 128), F32)
+        upper = [jnp.zeros((8, 128), F32)] * 8
         for p in range(0, 8, 2):
             q = p + 1
             first = {c: row_of(square[p], c) for c in range(p, 8)}
@@ -140,6 +143,8 @@
                 row = row_of(rows, k)
                 rows = rows - down * row
                 inverse = jnp.where(sub == k, inv, inverse)
+                for c in range(k + 1, 8) if b + NEAR[b] < 8 else ():
+                    upper[c] = jnp.where(sub == k, s[c], upper[c])
                 for i, panel in panels.items():
                     down = panel[k] * inv
                     for c in range(k + 1, 8):
@@ -149,6 +154,13 @@
                             following[c] = following[c] - down * row_of(panel[k], c)
                     a[i] = a[i] - down * row
         out_ref[8 * b : 8 * b + 8, :] = rows * (inverse * lax.rsqrt(inverse))
+        if b + NEAR[b] < 8:
+            q = rows * inverse
+            for c in range(7, 0, -1):
+                q = q - upper[c] * inverse * row_of(q, c)
+            q = [row_of(q, c) for c in range(8)]
+            for i in range(b + NEAR[b], 8):
+                a[i] = a[i] - tree([lanes_of(a[i], lane + c) * q[c] for c in range(8)])
         square = following
 
 

time: 82.4 us -> 82.1 us (level)
  no operation moved by 1% of the time
where the time goes in v6:
time: 82.1 us; the launch traced here: 81.8 us
  blocking collectives  48.1 us (59%)
  starting transfers between devices  15.9 us (19%)
  Pallas kernels  15 us (18%)
  waiting for transfers between devices  2.37 us (3%)
    all_to_all x2, blocking collectives, spread(): lax.all_to_all(jnp.broadcast_to(piece[None], (copies, *piece.shape)), axi...  33.8 us
    ppermute x2, starting transfers between devices, swap(): return lax.ppermute(value, 'core', [(0, 1), (1, 0)])  15.9 us
    all_to_all x1, blocking collectives, body(): lax.all_to_all(part.reshape(raster, 1, HALF * 128 // raster), 'raster', 0...  14.3 us
    pallas_call x1, Pallas kernels, finish(): pl.pallas_call(iterate_kernel, in_specs=[pl.BlockSpec(memory_space=pltpu....  10.9 us
    pallas_call x1, Pallas kernels, gram_halves(): pl.pallas_call(gram_kernel, in_specs=[pl.BlockSpec(memory_space=pltpu.SME...  4.05 us
    ppermute x2, waiting for transfers between devices, swap(): return lax.ppermute(value, 'core', [(0, 1), (1, 0)])  2.37 us
  transfers between devices with their start and end apart: 2, of which 2 were waited for; matrix products, arithmetic and copies ran while one was open for 0% of the time, Pallas kernels for 0%

profile of v6, /device:TPU:1, one launch (start us, length us, event | category | flops | bytes accessed | tf_op | source)
XLA Modules:
  0.0 81.8 jit_solution(3949544342717521270)
XLA Ops:
  0.0 0.0 copy-start
  0.0 4.0 %shard_map.28 = (f32[576,128]{1,0:T(8,128)S(1)}, f32[576,128]{1,0:T(8,128)S(1)}) custom-call(s32[1]{0:T(128)} %bitcast.core_ref, f32[2048,512]{1,0:T(8,128)} %spectra_ref.3), custom_call_target="tpu_custom_call" | custom-call | tf_op jit(solution)/shard_map/pallas_call | solution.py:85
  4.1 8.7 %collective-permute-start = (f32[576,128]{1,0:T(8,128)S(1)}, f32[576,128]{1,0:T(8,128)S(1)}, u32[]{:S(2)}, u32[]{:S(2)}) collective-permute-start(f32[576,128]{1,0:T(8,128)S(1)} %get-tuple-element.8), channel_id=1, source_target_pairs={{0,1},{1,0},{2,3},{3,2},{4,5},{5,4},{6,7},{7,6},{8,9},{9,8},{10,11... | collective-permute-start | bytes 884744 | tf_op jit(solution)/shard_map/ppermute | solution.py:259
  12.8 1.2 %collective-permute-done = f32[576,128]{1,0:T(8,128)S(1)} collective-permute-done((f32[576,128]{1,0:T(8,128)S(1)}, f32[576,128]{1,0:T(8,128)S(1)}, u32[]{:S(2)}, u32[]{:S(2)}) %collective-permute-start) | collective-permute-done | bytes 294944 | tf_op jit(solution)/shard_map/ppermute | solution.py:259
  14.0 14.3 %all_to_all.15 = f32[32,1,2304]{2,1,0:T(1,128)S(1)} all-to-all(f32[32,1,2304]{2,1,0:T(1,128)S(1)} %bitcast.8), channel_id=1, replica_groups=mesh['raster'=32,'z'=8,'core'=2] {'raster'}, dimensions={0} | all-to-all | bytes 589824 | tf_op jit(solution)/shard_map/all_to_all | solution.py:270
  28.3 0.2 reduce_sum.18
  28.5 17.1 %all_to_all.16 = f32[8,1,2304]{2,1,0:T(1,128)S(1)} all-to-all(f32[8,1,2304]{2,1,0:T(1,128)S(1)} %broadcast_in_dim.4), channel_id=1, replica_groups=mesh['raster'=32,'z'=8,'core'=2] {'z'}, dimensions={0} | all-to-all | bytes 147456 | tf_op jit(solution)/shard_map/all_to_all | solution.py:263
  45.7 0.1 reduce_sum.19
  45.7 0.2 broadcast_in_dim.5
  45.9 16.7 %all_to_all.17 = f32[32,1,2304]{2,1,0:T(1,128)S(1)} all-to-all(f32[32,1,2304]{2,1,0:T(1,128)S(1)} %broadcast_in_dim.5), channel_id=1, replica_groups=mesh['raster'=32,'z'=8,'core'=2] {'raster'}, dimensions={0} | all-to-all | bytes 589824 | tf_op jit(solution)/shard_map/all_to_all | solution.py:263
  62.6 7.2 %collective-permute-start.1 = (f32[576,128]{1,0:T(8,128)S(1)}, f32[576,128]{1,0:T(8,128)S(1)}, u32[]{:S(2)}, u32[]{:S(2)}) collective-permute-start(f32[576,128]{1,0:T(8,128)S(1)} %bitcast.5), channel_id=1, source_target_pairs={{0,1},{1,0},{2,3},{3,2},{4,5},{5,4},{6,7},{7,6},{8,9},{9,8},{10,11... | collective-permute-start | bytes 884744 | tf_op jit(solution)/shard_map/ppermute | solution.py:259
  69.7 1.2 %collective-permute-done.1.other_ref = f32[576,128]{1,0:T(8,128)S(1)} collective-permute-done((f32[576,128]{1,0:T(8,128)S(1)}, f32[576,128]{1,0:T(8,128)S(1)}, u32[]{:S(2)}, u32[]{:S(2)}) %collective-permute-start.1) | collective-permute-done | bytes 294944 | tf_op jit(solution)/shard_map/ppermute | solution.py:259
  70.9 0.0 copy-done
  70.9 10.9 %shard_map.29 = f32[64,2048]{1,0:T(8,128)} custom-call(s32[1]{0:T(128)} %bitcast.core_ref, f32[576,128]{1,0:T(8,128)S(1)} %bitcast.6, f32[576,128]{1,0:T(8,128)S(1)} %collective-permute-done.1.other_ref, f32[64,512]{1,0:T(8,128)S(1)} %bitcast.7, f32[2048,512]{1,0:T(8,128)} %spectra_ref.3), custom_call_target="tpu_custom_call" | custom-call | tf_op jit(solution)/shard_map/pallas_call | solution.py:239
  (2 shorter events, 0.1 us)
Async XLA Ops:
  0.0 70.9 %copy-start = (f32[512,64]{0,1:T(8,128)S(1)}, f32[512,64]{0,1:T(8,128)}, u32[]{:S(2)}) copy-start(f32[512,64]{0,1:T(8,128)} %param.3) | copy-start | bytes 393220
  4.1 9.9 %collective-permute-start = (f32[576,128]{1,0:T(8,128)S(1)}, f32[576,128]{1,0:T(8,128)S(1)}, u32[]{:S(2)}, u32[]{:S(2)}) collective-permute-start(f32[576,128]{1,0:T(8,128)S(1)} %get-tuple-element.8), channel_id=1, source_target_pairs={{0,1},{1,0},{2,3},{3,2},{4,5},{5,4},{6,7},{7,6},{8,9},{9,8},{10,11... | collective-permute-start | bytes 884744 | tf_op jit(solution)/shard_map/ppermute | solution.py:259
  62.6 8.3 %collective-permute-start.1 = (f32[576,128]{1,0:T(8,128)S(1)}, f32[576,128]{1,0:T(8,128)S(1)}, u32[]{:S(2)}, u32[]{:S(2)}) collective-permute-start(f32[576,128]{1,0:T(8,128)S(1)} %bitcast.5), channel_id=1, source_target_pairs={{0,1},{1,0},{2,3},{3,2},{4,5},{5,4},{6,7},{7,6},{8,9},{9,8},{10,11... | collective-permute-start | bytes 884744 | tf_op jit(solution)/shard_map/ppermute | solution.py:259

commit v7 on v6

--- a/solution.py
+++ b/solution.py
@@ -94,6 +94,35 @@
         ],
         compiler_params=pltpu.CompilerParams(vmem_limit_bytes=52 * 1024 * 1024),
     )(core, spectra)
+
+
+def split_kernel(part, after_ref, spectra_ref, high_ref, low_ref, buf, sems):
+    rows = buf.shape[0] // 4
+    loads = []
+    for n in range(4):
+        at = slice(n * rows, n * rows + rows)
+        start = part * buf.shape[0] + n * rows
+        loads.append((at, pltpu.make_async_copy(spectra_ref.at[start : start + rows], buf.at[at], sems.at[n])))
+        loads[-1][1].start()
+    for at, load in loads:
+        load.wait()
+        high_ref[at, :], low_ref[at, :] = split(buf[at, :])
+
+
+def split_part(part, after, spectra):
+    rows = spectra.shape[0] // 2
+    anywhere = pl.BlockSpec(memory_space=pl.ANY)
+    vmem = pl.BlockSpec(memory_space=pltpu.VMEM)
+    half = jax.ShapeDtypeStruct((rows, W), BF16)
+    return pl.pallas_call(
+        functools.partial(split_kernel, part),
+        in_specs=[anywhere, anywhere],
+        out_specs=[vmem, vmem],
+        out_shape=[half, half],
+        scratch_shapes=[pltpu.VMEM((rows, W), F32), pltpu.SemaphoreType.DMA((4,))],
+        cost_estimate=pl.CostEstimate(flops=4 * rows * W, bytes_accessed=8 * rows * W, transcendentals=0),
+        compiler_params=pltpu.CompilerParams(vmem_limit_bytes=52 * 1024 * 1024),
+    )(after, spectra)
 
 
 def tree(terms):
@@ -164,9 +193,13 @@
         square = following
 
 
-def iterate_kernel(core_ref, mine_ref, other_ref, start_ref, spectra_ref, out_ref, gh, gl, basis, rp, sbuf, obuf, sem, osem):
-    load = pltpu.make_async_copy(spectra_ref, sbuf, sem)
-    load.start()
+def iterate_kernel(core_ref, mine_ref, other_ref, start_ref, h0_ref, l0_ref, h1_ref, l1_ref, out_ref, gh, gl, basis, rp, sbuf, obuf, sem, osem):
+    half = sbuf.shape[1] // 2
+    loads = []
+    for n, ref in enumerate((h0_ref, l0_ref, h1_ref, l1_ref)):
+        at = slice(n // 2 * half, n // 2 * half + half)
+        loads.append(pltpu.make_async_copy(ref, sbuf.at[n % 2, at], sem.at[n]))
+        loads[-1].start()
     core = core_ref[0]
     zero_is_mine = core == 0
 
@@ -217,13 +250,14 @@
 
     lax.fori_loop(0, ITERS, step, 0)
     bh, bl = split(basis[...])
-    load.wait()
+    for load in loads:
+        load.wait()
     both = jnp.concatenate([bh, bl], axis=0)
     rows = 512
     stores = []
-    for i in range(sbuf.shape[0] // rows):
+    for i in range(sbuf.shape[1] // rows):
         at = slice(i * rows, i * rows + rows)
-        sh, sl = split(sbuf[at, :])
+        sh, sl = sbuf[0, at, :], sbuf[1, at, :]
         wide = mul(both, sh, NT)
         obuf[:, at] = wide[:K] + wide[K:] + mul(bh, sl, NT)
         stores.append(pltpu.make_async_copy(obuf.at[:, at], out_ref.at[:, at], osem.at[i]))
@@ -232,13 +266,13 @@
         store.wait()
 
 
-def finish(core, mine, other, start, spectra):
-    rows = spectra.shape[0]
+def finish(core, mine, other, start, *parts):
+    rows = 2 * parts[0].shape[0]
     vmem = pl.BlockSpec(memory_space=pltpu.VMEM)
     hbm = pl.BlockSpec(memory_space=pl.ANY)
     return pl.pallas_call(
         iterate_kernel,
-        in_specs=[pl.BlockSpec(memory_space=pltpu.SMEM), vmem, vmem, vmem, hbm],
+        in_specs=[pl.BlockSpec(memory_space=pltpu.SMEM), vmem, vmem, vmem, hbm, hbm, hbm, hbm],
         out_specs=hbm,
         out_shape=jax.ShapeDtypeStruct((K, rows), F32),
         scratch_shapes=[
@@ -246,13 +280,13 @@
             pltpu.VMEM((W, W), BF16),
             pltpu.VMEM((K, W), F32),
             pltpu.VMEM((K, 128), F32),
-            pltpu.VMEM((rows, W), F32),
+            pltpu.VMEM((2, rows, W), BF16),
             pltpu.VMEM((K, rows), F32),
-            pltpu.SemaphoreType.DMA,
+            pltpu.SemaphoreType.DMA((4,)),
             pltpu.SemaphoreType.DMA((rows // 512,)),
         ],
         compiler_params=pltpu.CompilerParams(vmem_limit_bytes=52 * 1024 * 1024),
-    )(core, mine, other, start, spectra)
+    )(core, mine, other, start, *parts)
 
 
 def swap(value):
@@ -266,12 +300,17 @@
 def body(raster, z, spectra, start):
     core = lax.axis_index("core").astype(jnp.int32).reshape(1)
     keep, send = gram_halves(core, spectra)
-    part = keep + swap(send)
+    arrived = swap(send)
+    early = split_part(0, send, spectra)
+    arrived, *early = lax.optimization_barrier((arrived, *early))
+    part = keep + arrived
     part = lax.all_to_all(part.reshape(raster, 1, HALF * 128 // raster), "raster", 0, 0)
     piece = jnp.sum(part, axis=0)
     piece = jnp.sum(spread(piece, "z", z), axis=0)
     mine = spread(piece, "raster", raster).reshape(HALF, 128)
-    return finish(core, mine, swap(mine), start.T, spectra).T
+    other = swap(mine)
+    late = split_part(1, mine, spectra)
+    return finish(core, mine, other, start.T, *early, *late).T
 
 
 def solution(mesh):

time: 82.1 us -> 85.5 us (1.041)
  Pallas kernels: 15 us -> 20.3 us
  waiting for transfers between devices: 2.37 us -> 0.01 us
  local copies, waits for them, and re-layouts: 0.2 us -> 1.18 us
    pallas_call x0 -> x2, Pallas kernels: none -> 5.22 us  [split_part(): pl.pallas_call(functools.partial(split_kernel, part), in_specs=[anywhere,...]
    ppermute x2, waiting for transfers between devices: 2.37 us -> 0.01 us  [swap(): return lax.ppermute(value, 'core', [(0, 1), (1, 0)])]
    unnamed x2 -> x4, local copies, waits for them, and re-layouts: 0.01 us -> 0.99 us
  transfers between devices with their start and end apart: 2 -> 2, of which waited for: 2 -> 0; matrix products, arithmetic and copies ran while one was open for 0% -> 0% of each run, Pallas kernels for 0% -> 6%
where the time goes in v7:
time: 85.5 us; the launch traced here: 85.2 us
  blocking collectives  48.3 us (56%)
  Pallas kernels  20.3 us (24%)
  starting transfers between devices  15.1 us (18%)
  local copies, waits for them, and re-layouts  1.18 us (1%)
    all_to_all x2, blocking collectives, spread(): lax.all_to_all(jnp.broadcast_to(piece[None], (copies, *piece.shape)), axi...  33.6 us
    ppermute x2, starting transfers between devices, swap(): return lax.ppermute(value, 'core', [(0, 1), (1, 0)])  15.1 us
    all_to_all x1, blocking collectives, body(): lax.all_to_all(part.reshape(raster, 1, HALF * 128 // raster), 'raster', 0...  14.7 us
    pallas_call x1, Pallas kernels, finish(): pl.pallas_call(iterate_kernel, in_specs=[pl.BlockSpec(memory_space=pltpu....  11 us
    pallas_call x2, Pallas kernels, split_part(): pl.pallas_call(functools.partial(split_kernel, part), in_specs=[anywhere,...  5.22 us
    pallas_call x1, Pallas kernels, gram_halves(): pl.pallas_call(gram_kernel, in_specs=[pl.BlockSpec(memory_space=pltpu.SME...  4.03 us
  transfers between devices with their start and end apart: 2, of which 0 were waited for; matrix products, arithmetic and copies ran while one was open for 0% of the time, Pallas kernels for 6%

profile of v7, /device:TPU:1, one launch (start us, length us, event | category | flops | bytes accessed | tf_op | source)
XLA Modules:
  0.0 85.2 jit_solution(4460288094904807147)
XLA Ops:
  0.0 4.0 %shard_map.28 = (f32[576,128]{1,0:T(8,128)S(1)}, f32[576,128]{1,0:T(8,128)S(1)}) custom-call(s32[1]{0:T(128)} %bitcast.core_ref, f32[2048,512]{1,0:T(8,128)} %spectra_ref.5), custom_call_target="tpu_custom_call" | custom-call | tf_op jit(solution)/shard_map/pallas_call | solution.py:85
  4.0 8.7 %collective-permute-start = (f32[576,128]{1,0:T(8,128)S(1)}, f32[576,128]{1,0:T(8,128)S(1)}, u32[]{:S(2)}, u32[]{:S(2)}) collective-permute-start(f32[576,128]{1,0:T(8,128)S(1)} %get-tuple-element.15.after_ref), channel_id=1, source_target_pairs={{0,1},{1,0},{2,3},{3,2},{4,5},{5,4},{6,7},{7,6},{8,9},{9,8},{10,11... | collective-permute-start | bytes 884744 | tf_op jit(solution)/shard_map/ppermute | solution.py:293
  12.8 2.6 %shard_map.29 = (bf16[1024,512]{1,0:T(8,128)(2,1)S(1)}, bf16[1024,512]{1,0:T(8,128)(2,1)}) custom-call(f32[576,128]{1,0:T(8,128)S(1)} %get-tuple-element.15.after_ref, f32[2048,512]{1,0:T(8,128)} %spectra_ref.5), custom_call_target="tpu_custom_call" | custom-call | flops 2097152 | bytes 4194304 | tf_op jit(solution)/shard_map/pallas_call | solution.py:117
  15.4 0.0 copy-start.1
  15.4 0.0 collective-permute-done
  15.4 14.7 %all_to_all.15 = f32[32,1,2304]{2,1,0:T(1,128)S(1)} all-to-all(f32[32,1,2304]{2,1,0:T(1,128)S(1)} %bitcast.9), channel_id=1, replica_groups=mesh['raster'=32,'z'=8,'core'=2] {'raster'}, dimensions={0} | all-to-all | bytes 589824 | tf_op jit(solution)/shard_map/all_to_all | solution.py:307
  30.1 0.2 reduce_sum.18
  30.4 17.3 %all_to_all.16 = f32[8,1,2304]{2,1,0:T(1,128)S(1)} all-to-all(f32[8,1,2304]{2,1,0:T(1,128)S(1)} %broadcast_in_dim.4), channel_id=1, replica_groups=mesh['raster'=32,'z'=8,'core'=2] {'z'}, dimensions={0} | all-to-all | bytes 147456 | tf_op jit(solution)/shard_map/all_to_all | solution.py:297
  47.6 0.1 reduce_sum.19
  47.7 0.2 broadcast_in_dim.5
  47.8 16.3 %all_to_all.17 = f32[32,1,2304]{2,1,0:T(1,128)S(1)} all-to-all(f32[32,1,2304]{2,1,0:T(1,128)S(1)} %broadcast_in_dim.5), channel_id=1, replica_groups=mesh['raster'=32,'z'=8,'core'=2] {'raster'}, dimensions={0} | all-to-all | bytes 589824 | tf_op jit(solution)/shard_map/all_to_all | solution.py:297
  64.2 6.4 %collective-permute-start.1 = (f32[576,128]{1,0:T(8,128)S(1)}, f32[576,128]{1,0:T(8,128)S(1)}, u32[]{:S(2)}, u32[]{:S(2)}) collective-permute-start(f32[576,128]{1,0:T(8,128)S(1)} %bitcast.5), channel_id=1, source_target_pairs={{0,1},{1,0},{2,3},{3,2},{4,5},{5,4},{6,7},{7,6},{8,9},{9,8},{10,11... | collective-permute-start | bytes 884744 | tf_op jit(solution)/shard_map/ppermute | solution.py:293
  70.5 2.6 %shard_map.30 = (bf16[1024,512]{1,0:T(8,128)(2,1)S(1)}, bf16[1024,512]{1,0:T(8,128)(2,1)}) custom-call(f32[576,128]{1,0:T(8,128)S(1)} %bitcast.6, f32[2048,512]{1,0:T(8,128)} %spectra_ref.5), custom_call_target="tpu_custom_call" | custom-call | flops 2097152 | bytes 4194304 | tf_op jit(solution)/shard_map/pallas_call | solution.py:117
  73.2 0.0 copy-start
  73.2 1.0 %copy-done = bf16[1024,512]{1,0:T(8,128)(2,1)} copy-done((bf16[1024,512]{1,0:T(8,128)(2,1)}, bf16[1024,512]{1,0:T(8,128)(2,1)S(1)}, u32[]{:S(2)}) %copy-start) | copy-done | bytes 1048600
  74.2 0.0 collective-permute-done.1.other_ref
  74.2 0.0 copy-done.1
  74.2 11.0 %shard_map.31 = f32[64,2048]{1,0:T(8,128)} custom-call(s32[1]{0:T(128)} %bitcast.core_ref, f32[576,128]{1,0:T(8,128)S(1)} %bitcast.7, f32[576,128]{1,0:T(8,128)S(1)} %collective-permute-done.1.other_ref, f32[64,512]{1,0:T(8,128)S(1)} %bitcast.8, bf16[1024,512]{1,0:T(8,128)(2,1)S(1)} %get-tuple-element.19.h0_ref, bf16[1024,512]{1,0:T(8,128)(2,1)} %get-tuple-element.20.l0_ref, ...), custom_call_target="tpu_custom_call" | custom-call | tf_op jit(solution)/shard_map/pallas_call | solution.py:273
  (2 shorter events, 0.1 us)
Async XLA Ops:
  4.0 11.3 %collective-permute-start = (f32[576,128]{1,0:T(8,128)S(1)}, f32[576,128]{1,0:T(8,128)S(1)}, u32[]{:S(2)}, u32[]{:S(2)}) collective-permute-start(f32[576,128]{1,0:T(8,128)S(1)} %get-tuple-element.15.after_ref), channel_id=1, source_target_pairs={{0,1},{1,0},{2,3},{3,2},{4,5},{5,4},{6,7},{7,6},{8,9},{9,8},{10,11... | collective-permute-start | bytes 884744 | tf_op jit(solution)/shard_map/ppermute | solution.py:293
  15.4 58.8 %copy-start.1 = (f32[512,64]{0,1:T(8,128)S(1)}, f32[512,64]{0,1:T(8,128)}, u32[]{:S(2)}) copy-start(f32[512,64]{0,1:T(8,128)} %param.3) | copy-start | bytes 393220
  64.2 10.0 %collective-permute-start.1 = (f32[576,128]{1,0:T(8,128)S(1)}, f32[576,128]{1,0:T(8,128)S(1)}, u32[]{:S(2)}, u32[]{:S(2)}) collective-permute-start(f32[576,128]{1,0:T(8,128)S(1)} %bitcast.5), channel_id=1, source_target_pairs={{0,1},{1,0},{2,3},{3,2},{4,5},{5,4},{6,7},{7,6},{8,9},{9,8},{10,11... | collective-permute-start | bytes 884744 | tf_op jit(solution)/shard_map/ppermute | solution.py:293
  73.2 1.0 %copy-start = (bf16[1024,512]{1,0:T(8,128)(2,1)}, bf16[1024,512]{1,0:T(8,128)(2,1)S(1)}, u32[]{:S(2)}) copy-start(bf16[1024,512]{1,0:T(8,128)(2,1)S(1)} %get-tuple-element.21.h1_ref) | copy-start | bytes 3145732

commit v8 on v6

--- a/solution.py
+++ b/solution.py
@@ -219,7 +219,7 @@
     bh, bl = split(basis[...])
     load.wait()
     both = jnp.concatenate([bh, bl], axis=0)
-    rows = 512
+    rows = 256
     stores = []
     for i in range(sbuf.shape[0] // rows):
         at = slice(i * rows, i * rows + rows)
@@ -249,7 +249,7 @@
             pltpu.VMEM((rows, W), F32),
             pltpu.VMEM((K, rows), F32),
             pltpu.SemaphoreType.DMA,
-            pltpu.SemaphoreType.DMA((rows // 512,)),
+            pltpu.SemaphoreType.DMA((rows // 256,)),
         ],
         compiler_params=pltpu.CompilerParams(vmem_limit_bytes=52 * 1024 * 1024),
     )(core, mine, other, start, spectra)

time: 82.1 us -> 82.1 us (level)
  no operation moved by 1% of the time
where the time goes in v8:
time: 82.1 us; the launch traced here: 81.9 us
  blocking collectives  48.1 us (59%)
  starting transfers between devices  15.9 us (19%)
  Pallas kernels  15 us (18%)
  waiting for transfers between devices  2.37 us (3%)
    all_to_all x2, blocking collectives, spread(): lax.all_to_all(jnp.broadcast_to(piece[None], (copies, *piece.shape)), axi...  33.8 us
    ppermute x2, starting transfers between devices, swap(): return lax.ppermute(value, 'core', [(0, 1), (1, 0)])  15.9 us
    all_to_all x1, blocking collectives, body(): lax.all_to_all(part.reshape(raster, 1, HALF * 128 // raster), 'raster', 0...  14.3 us
    pallas_call x1, Pallas kernels, finish(): pl.pallas_call(iterate_kernel, in_specs=[pl.BlockSpec(memory_space=pltpu....  11 us
    pallas_call x1, Pallas kernels, gram_halves(): pl.pallas_call(gram_kernel, in_specs=[pl.BlockSpec(memory_space=pltpu.SME...  4.05 us
    ppermute x2, waiting for transfers between devices, swap(): return lax.ppermute(value, 'core', [(0, 1), (1, 0)])  2.37 us
  transfers between devices with their start and end apart: 2, of which 2 were waited for; matrix products, arithmetic and copies ran while one was open for 0% of the time, Pallas kernels for 0%

profile of v8, /device:TPU:1, one launch (start us, length us, event | category | flops | bytes accessed | tf_op | source)
XLA Modules:
  0.0 81.9 jit_solution(10927334197843127832)
XLA Ops:
  0.0 0.0 copy-start
  0.0 4.0 %shard_map.28 = (f32[576,128]{1,0:T(8,128)S(1)}, f32[576,128]{1,0:T(8,128)S(1)}) custom-call(s32[1]{0:T(128)} %bitcast.core_ref, f32[2048,512]{1,0:T(8,128)} %spectra_ref.3), custom_call_target="tpu_custom_call" | custom-call | tf_op jit(solution)/shard_map/pallas_call | solution.py:85
  4.1 8.7 %collective-permute-start = (f32[576,128]{1,0:T(8,128)S(1)}, f32[576,128]{1,0:T(8,128)S(1)}, u32[]{:S(2)}, u32[]{:S(2)}) collective-permute-start(f32[576,128]{1,0:T(8,128)S(1)} %get-tuple-element.8), channel_id=1, source_target_pairs={{0,1},{1,0},{2,3},{3,2},{4,5},{5,4},{6,7},{7,6},{8,9},{9,8},{10,11... | collective-permute-start | bytes 884744 | tf_op jit(solution)/shard_map/ppermute | solution.py:259
  12.8 1.2 %collective-permute-done = f32[576,128]{1,0:T(8,128)S(1)} collective-permute-done((f32[576,128]{1,0:T(8,128)S(1)}, f32[576,128]{1,0:T(8,128)S(1)}, u32[]{:S(2)}, u32[]{:S(2)}) %collective-permute-start) | collective-permute-done | bytes 294944 | tf_op jit(solution)/shard_map/ppermute | solution.py:259
  14.0 14.3 %all_to_all.15 = f32[32,1,2304]{2,1,0:T(1,128)S(1)} all-to-all(f32[32,1,2304]{2,1,0:T(1,128)S(1)} %bitcast.8), channel_id=1, replica_groups=mesh['raster'=32,'z'=8,'core'=2] {'raster'}, dimensions={0} | all-to-all | bytes 589824 | tf_op jit(solution)/shard_map/all_to_all | solution.py:270
  28.3 0.2 reduce_sum.18
  28.5 17.1 %all_to_all.16 = f32[8,1,2304]{2,1,0:T(1,128)S(1)} all-to-all(f32[8,1,2304]{2,1,0:T(1,128)S(1)} %broadcast_in_dim.4), channel_id=1, replica_groups=mesh['raster'=32,'z'=8,'core'=2] {'z'}, dimensions={0} | all-to-all | bytes 147456 | tf_op jit(solution)/shard_map/all_to_all | solution.py:263
  45.7 0.1 reduce_sum.19
  45.7 0.2 broadcast_in_dim.5
  45.9 16.7 %all_to_all.17 = f32[32,1,2304]{2,1,0:T(1,128)S(1)} all-to-all(f32[32,1,2304]{2,1,0:T(1,128)S(1)} %broadcast_in_dim.5), channel_id=1, replica_groups=mesh['raster'=32,'z'=8,'core'=2] {'raster'}, dimensions={0} | all-to-all | bytes 589824 | tf_op jit(solution)/shard_map/all_to_all | solution.py:263
  62.6 7.2 %collective-permute-start.1 = (f32[576,128]{1,0:T(8,128)S(1)}, f32[576,128]{1,0:T(8,128)S(1)}, u32[]{:S(2)}, u32[]{:S(2)}) collective-permute-start(f32[576,128]{1,0:T(8,128)S(1)} %bitcast.5), channel_id=1, source_target_pairs={{0,1},{1,0},{2,3},{3,2},{4,5},{5,4},{6,7},{7,6},{8,9},{9,8},{10,11... | collective-permute-start | bytes 884744 | tf_op jit(solution)/shard_map/ppermute | solution.py:259
  69.7 1.2 %collective-permute-done.1.other_ref = f32[576,128]{1,0:T(8,128)S(1)} collective-permute-done((f32[576,128]{1,0:T(8,128)S(1)}, f32[576,128]{1,0:T(8,128)S(1)}, u32[]{:S(2)}, u32[]{:S(2)}) %collective-permute-start.1) | collective-permute-done | bytes 294944 | tf_op jit(solution)/shard_map/ppermute | solution.py:259
  70.9 0.0 copy-done
  70.9 11.0 %shard_map.29 = f32[64,2048]{1,0:T(8,128)} custom-call(s32[1]{0:T(128)} %bitcast.core_ref, f32[576,128]{1,0:T(8,128)S(1)} %bitcast.6, f32[576,128]{1,0:T(8,128)S(1)} %collective-permute-done.1.other_ref, f32[64,512]{1,0:T(8,128)S(1)} %bitcast.7, f32[2048,512]{1,0:T(8,128)} %spectra_ref.3), custom_call_target="tpu_custom_call" | custom-call | tf_op jit(solution)/shard_map/pallas_call | solution.py:239
  (2 shorter events, 0.1 us)
Async XLA Ops:
  0.0 70.9 %copy-start = (f32[512,64]{0,1:T(8,128)S(1)}, f32[512,64]{0,1:T(8,128)}, u32[]{:S(2)}) copy-start(f32[512,64]{0,1:T(8,128)} %param.3) | copy-start | bytes 393220
  4.1 9.9 %collective-permute-start = (f32[576,128]{1,0:T(8,128)S(1)}, f32[576,128]{1,0:T(8,128)S(1)}, u32[]{:S(2)}, u32[]{:S(2)}) collective-permute-start(f32[576,128]{1,0:T(8,128)S(1)} %get-tuple-element.8), channel_id=1, source_target_pairs={{0,1},{1,0},{2,3},{3,2},{4,5},{5,4},{6,7},{7,6},{8,9},{9,8},{10,11... | collective-permute-start | bytes 884744 | tf_op jit(solution)/shard_map/ppermute | solution.py:259
  62.6 8.3 %collective-permute-start.1 = (f32[576,128]{1,0:T(8,128)S(1)}, f32[576,128]{1,0:T(8,128)S(1)}, u32[]{:S(2)}, u32[]{:S(2)}) collective-permute-start(f32[576,128]{1,0:T(8,128)S(1)} %bitcast.5), channel_id=1, source_target_pairs={{0,1},{1,0},{2,3},{3,2},{4,5},{5,4},{6,7},{7,6},{8,9},{9,8},{10,11... | collective-permute-start | bytes 884744 | tf_op jit(solution)/shard_map/ppermute | solution.py:259
